TPU v7x, 32 devices: a whole 2x2x4 slice. The times are simulated.
32 devices in a mesh: dp: 4 (over z), row: 2 (over y), col: 4 (over x, core).
Axes of the slice: x: 2, y: 2, z: 4, core: 2. Of those that a mesh axis runs over, the one named last changes fastest.
Arguments:
- hidden: bfloat16 [1024, 14336], P(('dp', 'col'), 'row'), may hold values from -6 to 6
- weight_blocks: bfloat16 [2, 4, 320, 128, 128], P('row', 'col'), may hold values from -0.0625 to 0.0625
- kept_blocks: int32 [2, 4, 320], P('row', 'col'), may hold values from -1 to 447, as said below
- cotangent: bfloat16 [1024, 4096], P(('dp', 'row'), 'col'), may hold values from -6 to 6
Outputs:
- output: bfloat16 [1024, 4096], P(('dp', 'row'), 'col')
- input_grad: bfloat16 [1024, 14336], P(('dp', 'col'), 'row')
- weight_grad: bfloat16 [2, 4, 320, 128, 128], P('row', 'col', 'dp')
Inputs may be any that keep to these rules, and one draw needn't show every extreme that they name: `kept_blocks`: entry s of grid position (i, j) names a block of that position's region by its local index, local block row times C plus local block column, with C = 8; entries of one position are distinct; -1 marks an empty slot, and empty slots come after the used ones. Each position uses between R C - 320 and 320 slots, with R = 56; some position uses all 320.
All inputs are finite; a program needn't handle non-finite values.
Results may differ from a plain program's by a relative error of at most 0.009.
Values may be sent and summed in bfloat16 or wider, within the bound.
No kernel may reach another device: no remote copies, remote signals or barrier semaphores. Data moves between devices by JAX's collectives and lax.ppermute only.
A program may use at most 192 MiB of HBM per device.

v0:
```python
import jax
import jax.numpy as jnp
from jax import lax
from jax.sharding import PartitionSpec as P


def on_device(hidden, weight_blocks, kept_blocks, cotangent):
    block_size = weight_blocks.shape[-1]
    slot_count = weight_blocks.shape[2]
    blocks = weight_blocks.reshape(slot_count, block_size, block_size)
    chosen = kept_blocks.reshape(slot_count)
    usable = chosen >= 0
    row_blocks = hidden.shape[1] // block_size
    col_blocks = cotangent.shape[1] // block_size
    clamped = jnp.where(usable, chosen, 0)
    block_row = clamped // col_blocks
    block_col = clamped % col_blocks
    keep_mask = usable.astype(jnp.float32)
    masked = blocks * usable.astype(jnp.bfloat16)[:, None, None]
    row_onehot = (block_row[:, None] == jnp.arange(row_blocks)[None, :]) & usable[:, None]
    col_onehot = (block_col[:, None] == jnp.arange(col_blocks)[None, :]) & usable[:, None]
    gathered_hidden = lax.all_gather(hidden, "col", axis=0, tiled=True)
    gathered_grad = lax.all_gather(cotangent, "row", axis=0, tiled=True)
    tokens_all = gathered_hidden.shape[0]
    token_scale = 1.0 / tokens_all
    hidden_picked = jnp.take(
        gathered_hidden.reshape(tokens_all, row_blocks, block_size), block_row, axis=1
    )
    grad_picked = jnp.take(
        gathered_grad.reshape(tokens_all, col_blocks, block_size), block_col, axis=1
    )
    dense_region = jnp.einsum(
        "sa,sc,skn->akcn",
        row_onehot.astype(jnp.bfloat16),
        col_onehot.astype(jnp.bfloat16),
        masked,
        preferred_element_type=jnp.float32,
    ).astype(jnp.bfloat16)
    dense_region = dense_region.reshape(row_blocks * block_size, col_blocks * block_size)
    output_part = jnp.dot(gathered_hidden, dense_region, preferred_element_type=jnp.float32)
    input_part = lax.dot_general(
        gathered_grad, dense_region, (((1,), (1,)), ((), ())), preferred_element_type=jnp.float32
    )
    output_rounded = output_part.astype(jnp.bfloat16).reshape(1, tokens_all, -1)
    output_pieces = lax.all_to_all(output_rounded, "row", split_axis=1, concat_axis=0, tiled=True)
    output = jnp.sum(output_pieces.astype(jnp.float32), axis=0).astype(jnp.bfloat16)
    input_rounded = input_part.astype(jnp.bfloat16).reshape(1, tokens_all, -1)
    input_pieces = lax.all_to_all(input_rounded, "col", split_axis=1, concat_axis=0, tiled=True)
    input_grad = jnp.sum(input_pieces.astype(jnp.float32), axis=0).astype(jnp.bfloat16)
    product = jnp.einsum(
        "tsk,tsn->skn", hidden_picked, grad_picked, preferred_element_type=jnp.float32
    )
    weight_grad = lax.psum_scatter(
        (product * (keep_mask * token_scale)[:, None, None]).astype(jnp.bfloat16),
        "dp",
        scatter_dimension=0,
        tiled=True,
    ).astype(jnp.float32)
    weight_grad = weight_grad.astype(jnp.bfloat16).reshape(1, 1, -1, block_size, block_size)
    return (output, input_grad, weight_grad)


def solution(mesh):
    in_specs = (
        P(("dp", "col"), "row"),
        P("row", "col", None, None, None),
        P("row", "col", None),
        P(("dp", "row"), "col"),
    )
    out_specs = (
        P(("dp", "row"), "col"),
        P(("dp", "col"), "row"),
        P("row", "col", "dp", None, None),
    )
    return jax.shard_map(
        on_device, mesh=mesh, in_specs=in_specs, out_specs=out_specs, check_vma=False
    )
```

profile of v0, /device:TPU:0, one launch (start us, length us, event | category | flops | bytes accessed | tf_op | source)
XLA Modules:
  0.0 273.8 jit_solution(12402908005295022273)
XLA Ops:
  7.2 0.0 all-gather.2.cloned.1.call-start
  7.2 0.7 all-gather.2.cloned.1.call-update
  7.9 0.0 reduce-scatter.2.cloned.1.call-start
  7.9 1.1 copy.36
  9.1 10.0 %all_gather.7 = bf16[256,1024]{0,1:T(8,128)(2,1)S(1)} all-gather(bf16[128,1024]{0,1:T(8,128)(2,1)S(1)} %copy.36), channel_id=1, replica_groups=mesh['dp'=4,'row'=2,'col'=4] {'row'}, dimensions={0}, use_global_device_ids=true | all-gather | bytes 786432 | tf_op jit(solution)/shard_map/all_gather | solution.py:23
  19.0 0.3 copy.40
  19.3 0.7 reduce.6
  20.0 0.7 fusion.44
  20.8 11.2 %gather_fusion.1 = bf16[320,256,128]{2,1,0:T(8,128)(2,1)} fusion(bf16[256,8,128]{2,0,1:T(8,128)(2,1)S(1)} %copy.40, s32[1024]{0:T(1024)S(1)} %get-tuple-element.17), kind=kCustom, calls=%fused_computation.1 | custom fusion | bytes 41944320 | tf_op jit(solution)/shard_map/jit(_take)/gather | solution.py:29
  32.0 11.8 %all-gather.2.cloned.1.call-done = bf16[256,7168]{1,0:T(8,128)(2,1)} async-done(((bf16[64,7168]{1,0:T(8,128)(2,1)}), bf16[256,7168]{1,0:T(8,128)(2,1)}) %all-gather.2.cloned.1.call-update) | async-done | bytes 3670032 | tf_op jit(solution)/shard_map/all_gather | solution.py:22
  43.8 5.9 %copy.38 = bf16[256,7168]{0,1:T(8,128)(2,1)} copy(bf16[256,7168]{1,0:T(8,128)(2,1)} %all-gather.2.cloned.1.call-done) | data formatting | bytes 7340032 | tf_op jit(solution)/shard_map/all_gather | solution.py:22
  49.7 5.9 %copy.39 = bf16[256,56,128]{2,0,1:T(8,128)(2,1)} copy(bf16[256,56,128]{0,2,1:T(8,128)(2,1)} %bitcast.68) | data formatting | bytes 7340032 | tf_op jit(solution)/shard_map/reshape | solution.py:27
  55.6 13.4 %gather_fusion = bf16[320,256,128]{2,1,0:T(8,128)(2,1)} fusion(bf16[256,56,128]{2,0,1:T(8,128)(2,1)} %copy.39, s32[1024]{0:T(1024)S(1)} %get-tuple-element.18), kind=kCustom, calls=%fused_computation | custom fusion | bytes 41944320 | tf_op jit(solution)/shard_map/jit(_take)/gather | solution.py:26
  69.0 19.8 %multiply_convert_fusion = bf16[320,128,128]{2,1,0:T(8,128)(2,1)} fusion(f32[320]{0:T(512)S(1)} %broadcast_select_fusion, bf16[320,256,128]{2,1,0:T(8,128)(2,1)} %gather_fusion.1, pred[320]{0:T(512)(128)(4,1)S(1)} %get-tuple-element.14, bf16[320,256,128]{2,1,0:T(8,128)(2,1)} %gather_fusion, pred[320]{0:T(512)(128)(4,1)S(1)} %get-tuple-element.11), kind=kOutput, calls=%fused_computation.7 | convolution fusion | flops 2715811840 | bytes 52430720 | tf_op jit(solution)/shard_map/tsk,tsn->skn/dot_general | solution.py:50
  88.8 0.0 reduce-scatter.2.cloned.1.call-update
  88.8 10.4 %bitcast_multiply_fusion = bf16[320,128,128]{2,1,0:T(8,128)(2,1)} fusion(bf16[1,1,320,128,128]{4,3,2,1,0:T(8,128)(2,1)} %param.5, bf16[320]{0:T(512)(128)(2,1)S(1)} %get-tuple-element.16), kind=kLoop, calls=%fused_computation.19 | loop fusion | flops 5242880 | bytes 20972160 | tf_op jit(solution)/shard_map/mul | solution.py:19
  99.2 22.1 %convert_bitcast_fusion = bf16[56,128,8,128]{3,0,1,2:T(8,128)(2,1)} fusion(bf16[320,128,128]{2,1,0:T(8,128)(2,1)} %bitcast_multiply_fusion, f32[320,56]{0,1:T(8,128)S(1)} %fusion.40, f32[320,8]{0,1:T(8,128)S(1)} %fusion.42), kind=kOutput, calls=%fused_computation.14 | convolution fusion | flops 4705103872 | bytes 25247744 | tf_op jit(solution)/shard_map/sa,sc,skn->akcn/dot_general | solution.py:32
  121.4 13.1 %copy.33 = bf16[56,128,8,128]{3,2,1,0:T(8,128)(2,1)S(1)} copy(bf16[56,128,8,128]{3,0,1,2:T(8,128)(2,1)} %convert_bitcast_fusion) | data formatting | bytes 29360128 | tf_op jit(solution)/shard_map/convert_element_type | solution.py:38
  134.4 0.0 copy-start
  134.4 5.2 %copy-done = bf16[56,128,8,128]{3,2,1,0:T(8,128)(2,1)} copy-done((bf16[56,128,8,128]{3,2,1,0:T(8,128)(2,1)}, bf16[56,128,8,128]{3,2,1,0:T(8,128)(2,1)S(1)}, u32[]{:S(2)}) %copy-start) | copy-done | bytes 14680088
  139.7 5.5 %fusion.22 = bf16[1,256,7168]{1,2,0:T(8,128)(2,1)} fusion(bf16[256,1024]{0,1:T(8,128)(2,1)S(1)} %all_gather.7, bf16[896,8,8,128]{3,2,1,0:T(8,128)(2,1)S(1)} %bitcast.66), kind=kOutput, calls=%fused_computation.23 | convolution fusion | flops 3759931392 | bytes 18874368 | tf_op jit(solution)/shard_map/dot_general | solution.py:41
  145.2 16.4 %copy.37 = bf16[1,256,7168]{2,0,1:T(2,128)(2,1)} copy(bf16[1,256,7168]{1,2,0:T(8,128)(2,1)} %fusion.22) | data formatting | bytes 7340032 | tf_op jit(solution)/shard_map/reshape | solution.py:47
  161.5 0.5 broadcast.290
  162.0 23.3 %reduce.12 = bf16[256,7168]{1,0:T(8,128)(2,1)} reduce(bf16[256,1,7168]{2,1,0:T(2,128)(2,1)} %bitcast.64, bf16[]{:T(256)} %broadcast.290), dimensions={1}, to_apply=%bitcast.60.reduce_sub_computation | reduce | bytes 7340034
  185.3 5.7 %reshape.213 = bf16[4,2,229376]{2,1,0:T(2,128)(2,1)} reshape(bf16[256,7168]{1,0:T(8,128)(2,1)} %reduce.12) | data formatting | bytes 7340032
  191.1 4.7 %all-to-all-start.1 = ((bf16[4,2,229376]{2,1,0:T(2,128)(2,1)}), bf16[4,2,229376]{2,1,0:T(2,128)(2,1)}, u32[]{:S(2)}, u32[]{:S(2)}) async-start(bf16[4,2,229376]{2,1,0:T(2,128)(2,1)} %reshape.213), calls=%async_computation.1 | async-start | bytes 7340032 | tf_op jit(solution)/shard_map/all_to_all | solution.py:48
  195.8 10.5 %fusion.32 = bf16[1,256,1024]{1,2,0:T(8,128)(2,1)S(1)} fusion(bf16[256,7168]{1,0:T(8,128)(2,1)} %all-gather.2.cloned.1.call-done, bf16[896,8,8,128]{3,2,1,0:T(8,128)(2,1)} %bitcast.67), kind=kOutput, calls=%fused_computation.25 | convolution fusion | flops 3758358528 | bytes 18874368 | tf_op jit(solution)/shard_map/dot_general | solution.py:40
  206.3 1.0 copy.34
  207.3 3.7 %reduce.11 = bf16[256,1024]{1,0:T(8,128)(2,1)S(1)} reduce(bf16[256,1,1024]{2,1,0:T(2,128)(2,1)S(1)} %bitcast.71, bf16[]{:T(256)} %broadcast.290), dimensions={1}, to_apply=%bitcast.58.reduce_sub_computation | reduce | bytes 1048578
  211.0 1.1 reshape.211
  212.1 26.3 %all-to-all-done.1 = bf16[4,2,229376]{2,1,0:T(2,128)(2,1)} async-done(((bf16[4,2,229376]{2,1,0:T(2,128)(2,1)}), bf16[4,2,229376]{2,1,0:T(2,128)(2,1)}, u32[]{:S(2)}, u32[]{:S(2)}) %all-to-all-start.1) | async-done | bytes 3670048 | tf_op jit(solution)/shard_map/all_to_all | solution.py:48
  238.4 3.5 %all-to-all-start = ((bf16[2,2,65536]{2,1,0:T(2,128)(2,1)}), bf16[2,2,65536]{2,1,0:T(2,128)(2,1)S(1)}, u32[]{:S(2)}, u32[]{:S(2)}) async-start(bf16[2,2,65536]{2,1,0:T(2,128)(2,1)} %reshape.211), calls=%async_computation | async-start | bytes 1048576 | tf_op jit(solution)/shard_map/all_to_all | solution.py:45
  241.9 7.2 %reshape.214 = bf16[256,1,7168]{2,1,0:T(2,128)(2,1)} reshape(bf16[4,2,229376]{2,1,0:T(2,128)(2,1)} %all-to-all-done.1) | data formatting | bytes 7340032
  249.1 6.1 %copy.46 = bf16[1,256,7168]{2,1,0:T(8,128)(2,1)} copy(bf16[1,256,7168]{2,0,1:T(2,128)(2,1)} %bitcast.65) | data formatting | bytes 7340032
  255.2 3.8 %reduce_sum.25 = bf16[64,7168]{1,0:T(8,128)(2,1)} reduce(bf16[4,64,7168]{2,1,0:T(8,128)(2,1)} %bitcast.69, bf16[]{:T(256)} %constant.61.clone.1), dimensions={0}, to_apply=%region_1.2 | reduce | flops 1376256 | bytes 4587522 | tf_op jit(solution)/shard_map/reduce_sum | solution.py:49
  259.0 0.0 all-to-all-done
  259.0 0.5 reshape.212
  259.5 0.2 copy.45
  259.7 0.8 reduce_sum.24
  260.5 6.4 %reduce-scatter.2.cloned.1.call-done = bf16[80,128,128]{2,1,0:T(8,128)(2,1)} async-done(((bf16[320,128,128]{2,1,0:T(8,128)(2,1)}), bf16[80,128,128]{2,1,0:T(8,128)(2,1)}) %reduce-scatter.2.cloned.1.call-update) | async-done | bytes 2621456 | tf_op jit(solution)/shard_map/reduce_scatter | solution.py:53
  (6 shorter events, 0.1 us)
Async XLA Ops:
  7.2 36.6 %all-gather.2.cloned.1.call-start = ((), (), s32[]{:S(2)}) async-start(), calls=%async_computation.3 | async-start | bytes 4587520 | tf_op jit(solution)/shard_map/all_gather | solution.py:22
  7.9 259.0 %reduce-scatter.2.cloned.1.call-start = ((), (), s32[]{:S(2)}) async-start(), calls=%async_computation.4 | async-start | bytes 13107200 | tf_op jit(solution)/shard_map/reduce_scatter | solution.py:53
  134.4 5.2 %copy-start = (bf16[56,128,8,128]{3,2,1,0:T(8,128)(2,1)}, bf16[56,128,8,128]{3,2,1,0:T(8,128)(2,1)S(1)}, u32[]{:S(2)}) copy-start(bf16[56,128,8,128]{3,2,1,0:T(8,128)(2,1)S(1)} %copy.33) | copy-start | bytes 44040196
  191.1 47.4 %all-to-all-start.1 = ((bf16[4,2,229376]{2,1,0:T(2,128)(2,1)}), bf16[4,2,229376]{2,1,0:T(2,128)(2,1)}, u32[]{:S(2)}, u32[]{:S(2)}) async-start(bf16[4,2,229376]{2,1,0:T(2,128)(2,1)} %reshape.213), calls=%async_computation.1 | async-start | bytes 7340032 | tf_op jit(solution)/shard_map/all_to_all | solution.py:48
  238.4 20.6 %all-to-all-start = ((bf16[2,2,65536]{2,1,0:T(2,128)(2,1)}), bf16[2,2,65536]{2,1,0:T(2,128)(2,1)S(1)}, u32[]{:S(2)}, u32[]{:S(2)}) async-start(bf16[2,2,65536]{2,1,0:T(2,128)(2,1)} %reshape.211), calls=%async_computation | async-start | bytes 1048576 | tf_op jit(solution)/shard_map/all_to_all | solution.py:45
Sparse Core Ops, SparseCore 0:
  9.6 34.1 all-gather.1
  88.9 177.9 reduce-scatter.1
where the time goes:
time: 275 us; the launch traced here: 274 us
  local copies, waits for them, and re-layouts  94.7 us (34%)
  matrix products  57.9 us (21%)
  waiting for transfers between devices  45.2 us (16%)
  other arithmetic  43.5 us (16%)
  between operations  14.2 us (5%)
  blocking collectives  9.98 us (4%)
  starting transfers between devices  8.3 us (3%)
    unnamed x3, other arithmetic  27.7 us
    unnamed x10, local copies, waits for them, and re-layouts  27.6 us
    all_to_all x1, waiting for transfers between devices, on_device(): lax.all_to_all(input_rounded, 'col', split_axis=1, concat_axis=0, tiled=T...  26.3 us
    dot_general x1, matrix products, on_device(): jnp.einsum('sa,sc,skn->akcn', row_onehot.astype(jnp.bfloat16), col_onehot...  22.1 us
    dot_general x1, matrix products, on_device(): jnp.einsum('tsk,tsn->skn', hidden_picked, grad_picked, preferred_element_...  19.8 us
    reshape x1, local copies, waits for them, and re-layouts, on_device(): input_rounded = input_part.astype(jnp.bfloat16).reshape(1, tokens_all, -1)  16.4 us
    gather x1, local copies, waits for them, and re-layouts, on_device(): jnp.take(gathered_hidden.reshape(tokens_all, row_blocks, block_size), blo...  13.4 us
    convert_element_type x1, local copies, waits for them, and re-layouts, on_device(): dense_region = jnp.einsum('sa,sc,skn->akcn', row_onehot.astype(jnp.bfloat...  13.1 us
  transfers between devices with their start and end apart: 4, of which 3 were waited for; matrix products, arithmetic and copies ran while one was open for 53% of the time, Pallas kernels for 0%

commit v1 on v0

v1 whole, which is shorter than its diff:
```python
import functools

import jax
import jax.numpy as jnp
from jax import lax
from jax.experimental import pallas as pl
from jax.experimental.pallas import tpu as pltpu
from jax.sharding import PartitionSpec as P

VMEM = pltpu.VMEM
SMEM = pltpu.SMEM
LIMIT = 56 * 1024 * 1024


def whole(space):
    return pl.BlockSpec(memory_space=space)


def tile_of(size, most):
    best = 128
    for tile in range(128, most + 1, 128):
        if size % tile == 0:
            best = tile
    return best


def build_kernel(kept, blocks, dense):
    slots, block, _ = blocks.shape
    rows, cols = dense.shape
    col_blocks = cols // block

    def clear(index, carry):
        dense[pl.ds(pl.multiple_of(index * block, block), block), :] = jnp.zeros((block, cols), dense.dtype)
        return carry

    lax.fori_loop(0, rows // block, clear, 0)

    def place(slot, carry):
        chosen = kept[slot]

        @pl.when(chosen >= 0)
        def _():
            top = pl.multiple_of((chosen // col_blocks) * block, block)
            left = pl.multiple_of((chosen % col_blocks) * block, block)
            dense[pl.ds(top, block), pl.ds(left, block)] = blocks[slot]

        return carry

    lax.fori_loop(0, slots, place, 0)


def build_dense(kept, blocks, rows, cols):
    return pl.pallas_call(
        build_kernel,
        out_shape=jax.ShapeDtypeStruct((rows, cols), blocks.dtype),
        in_specs=[whole(SMEM), whole(VMEM)],
        out_specs=whole(VMEM),
        compiler_params=pltpu.CompilerParams(vmem_limit_bytes=LIMIT),
        cost_estimate=pl.CostEstimate(flops=0, bytes_accessed=2 * (blocks.size + rows * cols), transcendentals=0),
        name="build_dense",
    )(kept, blocks)


def input_kernel(grad, dense, keep, send):
    half = keep.shape[0]
    part = lax.dot_general(grad[...], dense[...], (((1,), (1,)), ((), ())), preferred_element_type=jnp.float32)
    keep[...] = part[:half].astype(keep.dtype)
    send[...] = part[half:].astype(send.dtype)


def input_partial(grad, dense):
    tokens, cols = grad.shape
    rows = dense.shape[0]
    tile = tile_of(rows, 512)
    shape = jax.ShapeDtypeStruct((tokens // 2, rows), grad.dtype)
    spec = pl.BlockSpec((tokens // 2, tile), lambda t: (0, t))
    return pl.pallas_call(
        input_kernel,
        grid=(rows // tile,),
        out_shape=(shape, shape),
        in_specs=[pl.BlockSpec((tokens, cols), lambda t: (0, 0)), pl.BlockSpec((tile, cols), lambda t: (t, 0))],
        out_specs=(spec, spec),
        compiler_params=pltpu.CompilerParams(vmem_limit_bytes=LIMIT),
        cost_estimate=pl.CostEstimate(
            flops=2 * tokens * rows * cols, bytes_accessed=2 * (rows * cols + tokens * (rows + cols)), transcendentals=0
        ),
        name="input_partial",
    )(grad, dense)


def output_kernel(count, order, *refs):
    pieces, dense, out, total = refs[:count], refs[count], refs[count + 1], refs[count + 2]
    step = pl.program_id(0)
    group = pieces[0].shape[0]
    hidden = jnp.concatenate([piece[...] for piece in pieces], axis=0)
    part = jnp.dot(hidden, dense[...], preferred_element_type=jnp.float32)

    @pl.when(step == 0)
    def _():
        total[...] = part

    @pl.when(step > 0)
    def _():
        total[...] += part

    @pl.when(step == pl.num_programs(0) - 1)
    def _():
        for index in range(count):
            start = pl.multiple_of(order[index] * group, group)
            out[pl.ds(start, group), :] = total[index * group:(index + 1) * group, :].astype(out.dtype)


def output_partial(order, pieces, dense):
    count = len(pieces)
    group, rows = pieces[0].shape
    tokens = group * count
    cols = dense.shape[1]
    tile = tile_of(rows, 512)
    return pl.pallas_call(
        functools.partial(output_kernel, count),
        grid=(rows // tile,),
        out_shape=jax.ShapeDtypeStruct((tokens, cols), pieces[0].dtype),
        in_specs=[whole(SMEM)]
        + [pl.BlockSpec((group, tile), lambda t: (0, t))] * count
        + [pl.BlockSpec((tile, cols), lambda t: (t, 0))],
        out_specs=pl.BlockSpec((tokens, cols), lambda t: (0, 0)),
        scratch_shapes=[pltpu.VMEM((tokens, cols), jnp.float32)],
        compiler_params=pltpu.CompilerParams(vmem_limit_bytes=LIMIT),
        cost_estimate=pl.CostEstimate(
            flops=2 * tokens * rows * cols, bytes_accessed=2 * (rows * cols + tokens * (rows + cols)), transcendentals=0
        ),
        name="output_partial",
    )(order, *pieces, dense)


def weight_kernel(count, first, last, scale, kept, *refs):
    pieces, turned = refs[:count], refs[count]
    before = None if first else refs[count + 1]
    out = refs[-1]
    slots, block, _ = out.shape
    col_blocks = turned.shape[0] // block

    def one(slot, carry):
        chosen = kept[slot]
        place = jnp.maximum(chosen, 0)
        top = pl.multiple_of((place // col_blocks) * block, block)
        left = pl.multiple_of((place % col_blocks) * block, block)
        hidden = jnp.concatenate([piece[:, pl.ds(top, block)] for piece in pieces], axis=0)
        part = jnp.dot(turned[pl.ds(left, block), :], hidden, preferred_element_type=jnp.float32)
        if not first:
            part = part + before[slot]
        if last:
            part = jnp.where(chosen >= 0, part * scale, 0.0).T
        out[slot] = part.astype(out.dtype)
        return carry

    lax.fori_loop(0, slots, one, 0, unroll=4 if slots % 4 == 0 else 1)


def weight_partial(kept, pieces, turned, before, block, scale, last):
    count = len(pieces)
    slots = kept.shape[0]
    first = before is None
    tokens = turned.shape[1]
    extra = () if first else (before,)
    kind = jnp.bfloat16 if last else jnp.float32
    return pl.pallas_call(
        functools.partial(weight_kernel, count, first, last, scale),
        out_shape=jax.ShapeDtypeStruct((slots, block, block), kind),
        in_specs=[whole(SMEM)] + [whole(VMEM)] * (count + 1 + len(extra)),
        out_specs=whole(VMEM),
        compiler_params=pltpu.CompilerParams(vmem_limit_bytes=LIMIT),
        cost_estimate=pl.CostEstimate(
            flops=8 * slots * tokens * block * block,
            bytes_accessed=2 * tokens * pieces[0].shape[1] + 8 * slots * block * block,
            transcendentals=0,
        ),
        name="weight_partial",
    )(kept, *pieces, turned, *extra)


def on_device(n_dp, n_row, n_col, hidden, weight_blocks, kept_blocks, cotangent):
    block = weight_blocks.shape[-1]
    slots = weight_blocks.shape[2]
    blocks = weight_blocks.reshape(slots, block, block)
    kept = kept_blocks.reshape(slots)
    group, rows = hidden.shape
    part_rows, cols = cotangent.shape
    tokens = group * n_col
    n_hi = n_col // 2
    dp, row, col = lax.axis_index("dp"), lax.axis_index("row"), lax.axis_index("col")
    share = slots // n_dp
    own_kept = lax.dynamic_slice_in_dim(kept, dp * share, share)
    hi, core = col // 2, col % 2
    mine = [((hi + step) % n_hi) * 2 + core for step in range(n_hi)]
    other = [((hi + step) % n_hi) * 2 + 1 - core for step in range(n_hi)]
    order = jnp.stack(mine + other).astype(jnp.int32)

    def shift(value, axis, size, step):
        return lax.ppermute(value, axis, [(index, (index + step) % size) for index in range(size)])

    def over_x(value, step):
        return lax.ppermute(
            value, "col", [(((index // 2 + step) % n_hi) * 2 + index % 2, index) for index in range(n_col)]
        )

    def to_x(value, step):
        return lax.ppermute(
            value, "col", [(index, ((index // 2 + step) % n_hi) * 2 + index % 2) for index in range(n_col)]
        )

    def swap(value):
        return lax.ppermute(value, "col", [(index, index ^ 1) for index in range(n_col)])

    def spread(value):
        near = [value] + [over_x(value, step) for step in range(1, n_hi)]
        return near + [swap(piece) for piece in near]

    def all_rows(value):
        held = [value] + [shift(value, "row", n_row, step) for step in range(1, n_row)]
        stacked = jnp.stack(held)
        return jnp.take(stacked, (row - jnp.arange(n_row)) % n_row, axis=0).reshape(tokens, cols)

    def arranged(value):
        return jnp.take(value.reshape(n_col, group, cols), order, axis=0).reshape(tokens, cols)

    grads = [arranged(all_rows(cotangent if step == 0 else shift(cotangent, "dp", n_dp, step))) for step in range(n_dp)]
    dense = build_dense(kept, blocks, rows, cols)

    keep, send = input_partial(grads[0], dense)
    got = swap(send)
    pair = (keep.astype(jnp.float32) + got.astype(jnp.float32)).reshape(n_hi, group, rows)
    input_grad = pair[0]
    for step in range(1, n_hi):
        input_grad = input_grad + to_x(pair[step].astype(jnp.bfloat16), step).astype(jnp.float32)
    input_grad = input_grad.astype(jnp.bfloat16)

    own = spread(hidden)
    part = output_partial(order, own, dense).reshape(n_row, part_rows, cols)
    output = lax.dynamic_index_in_dim(part, row, 0, keepdims=False).astype(jnp.float32)
    for step in range(1, n_row):
        piece = lax.dynamic_index_in_dim(part, (row + step) % n_row, 0, keepdims=False)
        output = output + shift(piece, "row", n_row, step).astype(jnp.float32)
    output = output.astype(jnp.bfloat16)

    total = None
    visits = [0] + sorted(range(1, n_dp), key=lambda step: min(step, n_dp - step))
    for place, step in enumerate(visits):
        pieces = own if step == 0 else spread(shift(hidden, "dp", n_dp, step))
        total = weight_partial(
            own_kept, pieces, grads[step].T, total, block, 1.0 / tokens, place == n_dp - 1
        )
    return output, input_grad, total.reshape(1, 1, share, block, block)


def solution(mesh):
    in_specs = (
        P(("dp", "col"), "row"),
        P("row", "col", None, None, None),
        P("row", "col", None),
        P(("dp", "row"), "col"),
    )
    out_specs = (
        P(("dp", "row"), "col"),
        P(("dp", "col"), "row"),
        P("row", "col", "dp", None, None),
    )
    sizes = (mesh.shape["dp"], mesh.shape["row"], mesh.shape["col"])
    return jax.shard_map(
        functools.partial(on_device, *sizes), mesh=mesh, in_specs=in_specs, out_specs=out_specs, check_vma=False
    )
```

time: 275 us -> 215 us (0.78)
  the two profiles are of different devices: /device:TPU:0 before, /device:TPU:24 now
where the time goes in v1:
time: 215 us; the launch traced here: 213 us
  Pallas kernels  89.8 us (42%)
  waiting for transfers between devices  83.6 us (39%)
  starting transfers between devices  15 us (7%)
  local copies, waits for them, and re-layouts  15 us (7%)
  other arithmetic  8.76 us (4%)
    ppermute x11, waiting for transfers between devices, shift(): lax.ppermute(value, axis, [(index, (index + step) % size) for index in ra...  59.8 us
    pallas_call x4, Pallas kernels, weight_partial(): pl.pallas_call(functools.partial(weight_kernel, count, first, last, scale...  43.1 us
    ppermute x4, waiting for transfers between devices, over_x(): lax.ppermute(value, 'col', [((index // 2 + step) % n_hi * 2 + index % 2,...  20.4 us
    pallas_call x1, Pallas kernels, build_dense(): pl.pallas_call(build_kernel, out_shape=jax.ShapeDtypeStruct((rows, cols),...  17.3 us
    pallas_call x1, Pallas kernels, output_partial(): pl.pallas_call(functools.partial(output_kernel, count), grid=(rows // til...  15.2 us
    pallas_call x1, Pallas kernels, input_partial(): pl.pallas_call(input_kernel, grid=(rows // tile,), out_shape=(shape, shap...  14.3 us
    ppermute x11, starting transfers between devices, shift(): lax.ppermute(value, axis, [(index, (index + step) % size) for index in ra...  7.88 us
    gather x4, local copies, waits for them, and re-layouts, arranged(): jnp.take(value.reshape(n_col, group, cols), order, axis=0)  5.2 us
  transfers between devices with their start and end apart: 25, of which 8 were waited for; matrix products, arithmetic and copies ran while one was open for 10% of the time, Pallas kernels for 42%

profile of v1, /device:TPU:24, one launch (start us, length us, event | category | flops | bytes accessed | tf_op | source)
XLA Modules:
  0.0 213.0 jit_solution(8548893774407964063)
XLA Ops:
  0.6 0.1 collective-permute-start.23
  0.7 1.9 collective-permute-start.11
  2.6 0.4 collective-permute-start.17
  3.0 1.5 collective-permute-start.4
  4.6 1.5 collective-permute-start
  6.1 0.1 compare_and_fusion
  6.2 3.1 %collective-permute-done.23 = bf16[128,1024]{1,0:T(8,128)(2,1)S(1)} collective-permute-done((bf16[128,1024]{1,0:T(8,128)(2,1)}, bf16[128,1024]{1,0:T(8,128)(2,1)S(1)}, u32[]{:S(2)}, u32[]{:S(2)}) %collective-permute-start.23) | collective-permute-done | bytes 262176 | tf_op jit(solution)/shard_map/ppermute | solution.py:200
  9.3 1.5 collective-permute-start.24
  10.8 14.8 %collective-permute-done.11 = bf16[128,1024]{1,0:T(8,128)(2,1)S(1)} collective-permute-done((bf16[128,1024]{1,0:T(8,128)(2,1)}, bf16[128,1024]{1,0:T(8,128)(2,1)S(1)}, u32[]{:S(2)}, u32[]{:S(2)}) %collective-permute-start.11) | collective-permute-done | bytes 262176 | tf_op jit(solution)/shard_map/ppermute | solution.py:200
  25.7 1.5 collective-permute-start.12
  27.2 1.3 reduce.kept
  28.5 17.3 %build_dense.1.refs_4_.dense = bf16[7168,1024]{1,0:T(8,128)(2,1)} custom-call(s32[320]{0:T(512)} %reduce.kept, bf16[320,128,128]{2,1,0:T(8,128)(2,1)} %bitcast.34), custom_call_target="tpu_custom_call" | custom-call | bytes 25165824 | tf_op jit(solution)/shard_map/build_dense/pallas_call | solution.py:53
  45.8 0.0 collective-permute-start.1
  45.8 0.4 collective-permute-start.18
  46.2 0.1 pad_maximum_fusion
  46.2 0.6 gather_fusion
  46.8 0.1 collective-permute-start.7
  46.9 0.1 pad_maximum_fusion.3
  47.0 0.6 gather_fusion.6
  47.6 0.1 collective-permute-start.13
  47.6 0.1 pad_maximum_fusion.1
  47.7 0.6 gather_fusion.2
  48.3 6.2 %collective-permute-done.18 = bf16[128,1024]{1,0:T(8,128)(2,1)S(1)} collective-permute-done((bf16[128,1024]{1,0:T(8,128)(2,1)S(1)}, bf16[128,1024]{1,0:T(8,128)(2,1)S(1)}, u32[]{:S(2)}, u32[]{:S(2)}) %collective-permute-start.18) | collective-permute-done | bytes 262176 | tf_op jit(solution)/shard_map/ppermute | solution.py:200
  54.5 0.0 collective-permute-start.19
  54.5 0.1 pad_maximum_fusion.2
  54.6 0.6 gather_fusion.4
  55.2 1.2 broadcast_select_fusion.4
  56.4 1.6 gather_fusion.7
  58.0 0.6 gather_fusion.3
  58.6 1.6 gather_fusion.5
  60.2 1.4 gather_fusion.1
  61.6 2.1 broadcast_select_fusion
  63.7 14.3 %input_partial.1 = (bf16[128,7168]{1,0:T(8,128)(2,1)}, bf16[128,7168]{1,0:T(8,128)(2,1)}) custom-call(bf16[256,1024]{1,0:T(8,128)(2,1)} %bitcast.35, bf16[7168,1024]{1,0:T(8,128)(2,1)} %build_dense.1.refs_4_.dense), custom_call_target="tpu_custom_call" | custom-call | flops 3758096384 | bytes 18874368 | tf_op jit(solution)/shard_map/input_partial/pallas_call | solution.py:77
  78.0 0.5 collective-permute-start.5
  78.5 28.6 %collective-permute-done.7.refs_0_ = bf16[64,7168]{1,0:T(8,128)(2,1)} collective-permute-done((bf16[64,7168]{1,0:T(8,128)(2,1)}, bf16[64,7168]{1,0:T(8,128)(2,1)}, u32[]{:S(2)}, u32[]{:S(2)}) %collective-permute-start.7) | collective-permute-done | bytes 917536 | tf_op jit(solution)/shard_map/ppermute | solution.py:200
  107.1 1.0 collective-permute-start.8
  108.1 1.0 collective-permute-start.14
  109.1 7.0 %collective-permute-done.19.refs_0_ = bf16[64,7168]{1,0:T(8,128)(2,1)} collective-permute-done((bf16[64,7168]{1,0:T(8,128)(2,1)}, bf16[64,7168]{1,0:T(8,128)(2,1)}, u32[]{:S(2)}, u32[]{:S(2)}) %collective-permute-start.19) | collective-permute-done | bytes 917536 | tf_op jit(solution)/shard_map/ppermute | solution.py:200
  116.1 1.0 collective-permute-start.20
  117.1 15.2 %output_partial.1 = bf16[256,1024]{1,0:T(8,128)(2,1)} custom-call(s32[4]{0:T(128)} %copy-done.7, bf16[64,7168]{1,0:T(8,128)(2,1)} %refs_0_.3, bf16[64,7168]{1,0:T(8,128)(2,1)} %collective-permute-done.refs_1_, bf16[64,7168]{1,0:T(8,128)(2,1)} %collective-permute-done.1.refs_2_, bf16[64,7168]{1,0:T(8,128)(2,1)} %collective-permute-done.2.refs_3_, ...), custom_call_target="tpu_custom_call" | custom-call | flops 3758096384 | bytes 18874368 | tf_op jit(solution)/shard_map/output_partial/pallas_call | solution.py:119
  132.3 1.0 dynamic-slice_bitcast_fusion
  133.2 0.0 copy-start.3
  133.3 0.4 collective-permute-start.3
  133.7 1.3 fusion.2.kept
  135.0 1.0 copy.11
  136.0 1.0 copy.8
  137.1 1.0 copy.9
  138.1 1.0 copy.10
  139.1 9.5 %weight_partial.4.refs_5_ = f32[80,128,128]{2,1,0:T(8,128)} custom-call(s32[80]{0:T(128)} %fusion.2.kept, bf16[64,7168]{1,0:T(8,128)(2,1)} %refs_0_.3, bf16[64,7168]{1,0:T(8,128)(2,1)} %collective-permute-done.refs_1_, bf16[64,7168]{1,0:T(8,128)(2,1)} %collective-permute-done.1.refs_2_, bf16[64,7168]{1,0:T(8,128)(2,1)} %collective-permute-done.2.refs_3_, ...), custom_call_target="tpu_custom_call" | custom-call | flops 2684354560 | bytes 14155776 | tf_op jit(solution)/shard_map/weight_partial/pallas_call | solution.py:167
  148.6 1.7 collective-permute-done.14.refs_1_
  150.3 18.7 %collective-permute-done.20.refs_1_ = bf16[64,7168]{1,0:T(8,128)(2,1)} collective-permute-done((bf16[64,7168]{1,0:T(8,128)(2,1)}, bf16[64,7168]{1,0:T(8,128)(2,1)}, u32[]{:S(2)}, u32[]{:S(2)}) %collective-permute-start.20) | collective-permute-done | bytes 917536 | tf_op jit(solution)/shard_map/ppermute | solution.py:203
  169.0 0.5 collective-permute-start.10
  169.5 0.1 collective-permute-start.16
  169.5 0.4 collective-permute-start.22
  170.0 2.0 convert_add_fusion
  172.0 0.1 slice.33
  172.1 3.5 %collective-permute-done.22.refs_3_ = bf16[64,7168]{1,0:T(8,128)(2,1)S(1)} collective-permute-done((bf16[64,7168]{1,0:T(8,128)(2,1)}, bf16[64,7168]{1,0:T(8,128)(2,1)S(1)}, u32[]{:S(2)}, u32[]{:S(2)}) %collective-permute-start.22) | collective-permute-done | bytes 917536 | tf_op jit(solution)/shard_map/ppermute | solution.py:213
  175.6 1.0 collective-permute-start.6
  176.6 0.8 fusion.1
  177.4 11.0 %weight_partial.5.refs_5_ = f32[80,128,128]{2,1,0:T(8,128)} custom-call(s32[80]{0:T(128)} %fusion.2.kept, bf16[64,7168]{1,0:T(8,128)(2,1)} %collective-permute-done.19.refs_0_, bf16[64,7168]{1,0:T(8,128)(2,1)} %collective-permute-done.20.refs_1_, bf16[64,7168]{1,0:T(8,128)(2,1)} %collective-permute-done.21.refs_2_, bf16[64,7168]{1,0:T(8,128)(2,1)} %copy-done.5, ...), custom_call_target="tpu_custom_call" | custom-call | flops 2684354560 | bytes 14155776 | tf_op jit(solution)/shard_map/weight_partial/pallas_call | solution.py:167
  188.4 11.0 %weight_partial.6.refs_5_ = f32[80,128,128]{2,1,0:T(8,128)} custom-call(s32[80]{0:T(128)} %fusion.2.kept, bf16[64,7168]{1,0:T(8,128)(2,1)} %collective-permute-done.13.refs_0_, bf16[64,7168]{1,0:T(8,128)(2,1)} %collective-permute-done.14.refs_1_, bf16[64,7168]{1,0:T(8,128)(2,1)} %collective-permute-done.15.refs_2_, ...), custom_call_target="tpu_custom_call" | custom-call | flops 2684354560 | bytes 14155776 | tf_op jit(solution)/shard_map/weight_partial/pallas_call | solution.py:167
  199.5 0.9 copy-done.4
  200.4 11.6 %weight_partial.7 = bf16[80,128,128]{2,1,0:T(8,128)(2,1)} custom-call(s32[80]{0:T(128)} %fusion.2.kept, bf16[64,7168]{1,0:T(8,128)(2,1)} %collective-permute-done.7.refs_0_, bf16[64,7168]{1,0:T(8,128)(2,1)} %copy-done.3, bf16[64,7168]{1,0:T(8,128)(2,1)} %copy-done.4, bf16[64,7168]{1,0:T(8,128)(2,1)} %collective-permute-done.10.refs_3_, ...), custom_call_target="tpu_custom_call" | custom-call | flops 2684354560 | bytes 14155776 | tf_op jit(solution)/shard_map/weight_partial/pallas_call | solution.py:167
  211.9 1.1 fusion
  (40 shorter events, 0.1 us)
Async XLA Ops:
  0.6 8.7 %collective-permute-start.23 = (bf16[128,1024]{1,0:T(8,128)(2,1)}, bf16[128,1024]{1,0:T(8,128)(2,1)S(1)}, u32[]{:S(2)}, u32[]{:S(2)}) collective-permute-start(bf16[128,1024]{1,0:T(8,128)(2,1)} %param.11), channel_id=1, source_target_pairs={{0,8},{8,16},{16,24},{24,0},{1,9},{9,17},{17,25},{25,1},{2,10},{10... | collective-permute-start | bytes 786440 | tf_op jit(solution)/shard_map/ppermute | solution.py:200
  0.7 25.0 %collective-permute-start.11 = (bf16[128,1024]{1,0:T(8,128)(2,1)}, bf16[128,1024]{1,0:T(8,128)(2,1)S(1)}, u32[]{:S(2)}, u32[]{:S(2)}) collective-permute-start(bf16[128,1024]{1,0:T(8,128)(2,1)} %param.11), channel_id=1, source_target_pairs={{0,16},{8,24},{16,0},{24,8},{1,17},{9,25},{17,1},{25,9},{2,18},{10... | collective-permute-start | bytes 786440 | tf_op jit(solution)/shard_map/ppermute | solution.py:200
  2.6 43.2 %collective-permute-start.17 = (bf16[128,1024]{1,0:T(8,128)(2,1)}, bf16[128,1024]{1,0:T(8,128)(2,1)S(1)}, u32[]{:S(2)}, u32[]{:S(2)}) collective-permute-start(bf16[128,1024]{1,0:T(8,128)(2,1)} %param.11), channel_id=1, source_target_pairs={{0,24},{8,0},{16,8},{24,16},{1,25},{9,1},{17,9},{25,17},{2,26},{10... | collective-permute-start | bytes 786440 | tf_op jit(solution)/shard_map/ppermute | solution.py:200
  3.0 42.7 %collective-permute-start.4 = (bf16[128,1024]{1,0:T(8,128)(2,1)}, bf16[128,1024]{1,0:T(8,128)(2,1)S(1)}, u32[]{:S(2)}, u32[]{:S(2)}) collective-permute-start(bf16[128,1024]{1,0:T(8,128)(2,1)} %param.11), channel_id=1, source_target_pairs={{0,4},{4,0},{1,5},{5,1},{2,6},{6,2},{3,7},{7,3},{8,12},{12,8},{9,1... | collective-permute-start | bytes 786440 | tf_op jit(solution)/shard_map/ppermute | solution.py:200
  4.6 59.1 %collective-permute-start = (bf16[64,7168]{1,0:T(8,128)(2,1)}, bf16[64,7168]{1,0:T(8,128)(2,1)}, u32[]{:S(2)}, u32[]{:S(2)}) collective-permute-start(bf16[64,7168]{1,0:T(8,128)(2,1)} %refs_0_.3), channel_id=1, source_target_pairs={{2,0},{3,1},{0,2},{1,3},{6,4},{7,5},{4,6},{5,7},{10,8},{11,9},{8,1... | collective-permute-start | bytes 2752520 | tf_op jit(solution)/shard_map/ppermute | solution.py:203
  6.1 39.6 %copy-start.7 = (s32[4]{0:T(128)}, s32[4]{0:T(128)S(1)}, u32[]{:S(2)}) copy-start(s32[4]{0:T(128)S(1)} %get-tuple-element.10.order) | copy-start | bytes 52
  9.3 37.5 %collective-permute-start.24 = (bf16[128,1024]{1,0:T(8,128)(2,1)S(1)}, bf16[128,1024]{1,0:T(8,128)(2,1)S(1)}, u32[]{:S(2)}, u32[]{:S(2)}) collective-permute-start(bf16[128,1024]{1,0:T(8,128)(2,1)S(1)} %collective-permute-done.23), channel_id=1, source_target_pairs={{0,4},{4,0},{1,5},{5,1},{2,6},{6,2},{3,7},{7,3},{8,12},{12,8},{9,1... | collective-permute-start | bytes 786440 | tf_op jit(solution)/shard_map/ppermute | solution.py:200
  25.7 21.9 %collective-permute-start.12 = (bf16[128,1024]{1,0:T(8,128)(2,1)S(1)}, bf16[128,1024]{1,0:T(8,128)(2,1)S(1)}, u32[]{:S(2)}, u32[]{:S(2)}) collective-permute-start(bf16[128,1024]{1,0:T(8,128)(2,1)S(1)} %collective-permute-done.11), channel_id=1, source_target_pairs={{0,4},{4,0},{1,5},{5,1},{2,6},{6,2},{3,7},{7,3},{8,12},{12,8},{9,1... | collective-permute-start | bytes 786440 | tf_op jit(solution)/shard_map/ppermute | solution.py:200
  28.5 17.7 %copy-start.6 = (bf16[128,1024]{1,0:T(8,128)(2,1)S(1)}, bf16[128,1024]{1,0:T(8,128)(2,1)}, u32[]{:S(2)}) copy-start(bf16[128,1024]{1,0:T(8,128)(2,1)} %param.11) | copy-start | bytes 786436
  45.8 32.2 %collective-permute-start.1 = (bf16[64,7168]{1,0:T(8,128)(2,1)}, bf16[64,7168]{1,0:T(8,128)(2,1)}, u32[]{:S(2)}, u32[]{:S(2)}) collective-permute-start(bf16[64,7168]{1,0:T(8,128)(2,1)} %refs_0_.3), channel_id=1, source_target_pairs={{0,1},{1,0},{2,3},{3,2},{4,5},{5,4},{6,7},{7,6},{8,9},{9,8},{10,11... | collective-permute-start | bytes 2752520 | tf_op jit(solution)/shard_map/ppermute | solution.py:213
  45.8 8.7 %collective-permute-start.18 = (bf16[128,1024]{1,0:T(8,128)(2,1)S(1)}, bf16[128,1024]{1,0:T(8,128)(2,1)S(1)}, u32[]{:S(2)}, u32[]{:S(2)}) collective-permute-start(bf16[128,1024]{1,0:T(8,128)(2,1)S(1)} %collective-permute-done.17), channel_id=1, source_target_pairs={{0,4},{4,0},{1,5},{5,1},{2,6},{6,2},{3,7},{7,3},{8,12},{12,8},{9,1... | collective-permute-start | bytes 786440 | tf_op jit(solution)/shard_map/ppermute | solution.py:200
  46.8 60.3 %collective-permute-start.7 = (bf16[64,7168]{1,0:T(8,128)(2,1)}, bf16[64,7168]{1,0:T(8,128)(2,1)}, u32[]{:S(2)}, u32[]{:S(2)}) collective-permute-start(bf16[64,7168]{1,0:T(8,128)(2,1)} %refs_0_.3), channel_id=1, source_target_pairs={{0,16},{8,24},{16,0},{24,8},{1,17},{9,25},{17,1},{25,9},{2,18},{10... | collective-permute-start | bytes 2752520 | tf_op jit(solution)/shard_map/ppermute | solution.py:200
  47.6 60.6 %collective-permute-start.13 = (bf16[64,7168]{1,0:T(8,128)(2,1)}, bf16[64,7168]{1,0:T(8,128)(2,1)}, u32[]{:S(2)}, u32[]{:S(2)}) collective-permute-start(bf16[64,7168]{1,0:T(8,128)(2,1)} %refs_0_.3), channel_id=1, source_target_pairs={{0,24},{8,0},{16,8},{24,16},{1,25},{9,1},{17,9},{25,17},{2,26},{10... | collective-permute-start | bytes 2752520 | tf_op jit(solution)/shard_map/ppermute | solution.py:200
  54.5 61.6 %collective-permute-start.19 = (bf16[64,7168]{1,0:T(8,128)(2,1)}, bf16[64,7168]{1,0:T(8,128)(2,1)}, u32[]{:S(2)}, u32[]{:S(2)}) collective-permute-start(bf16[64,7168]{1,0:T(8,128)(2,1)} %refs_0_.3), channel_id=1, source_target_pairs={{0,8},{8,16},{16,24},{24,0},{1,9},{9,17},{17,25},{25,1},{2,10},{10... | collective-permute-start | bytes 2752520 | tf_op jit(solution)/shard_map/ppermute | solution.py:200
  63.7 53.3 %collective-permute-start.2 = (bf16[64,7168]{1,0:T(8,128)(2,1)}, bf16[64,7168]{1,0:T(8,128)(2,1)}, u32[]{:S(2)}, u32[]{:S(2)}) collective-permute-start(bf16[64,7168]{1,0:T(8,128)(2,1)} %collective-permute-done.refs_1_), channel_id=1, source_target_pairs={{0,1},{1,0},{2,3},{3,2},{4,5},{5,4},{6,7},{7,6},{8,9},{9,8},{10,11... | collective-permute-start | bytes 2752520 | tf_op jit(solution)/shard_map/ppermute | solution.py:213
  78.0 91.6 %collective-permute-start.5 = (bf16[128,7168]{1,0:T(8,128)(2,1)}, bf16[128,7168]{1,0:T(8,128)(2,1)}, u32[]{:S(2)}, u32[]{:S(2)}) collective-permute-start(bf16[128,7168]{1,0:T(8,128)(2,1)} %get-tuple-element.8), channel_id=1, source_target_pairs={{0,1},{1,0},{2,3},{3,2},{4,5},{5,4},{6,7},{7,6},{8,9},{9,8},{10,11... | collective-permute-start | bytes 5505032 | tf_op jit(solution)/shard_map/ppermute | solution.py:213
  107.1 26.2 %collective-permute-start.8 = (bf16[64,7168]{1,0:T(8,128)(2,1)}, bf16[64,7168]{1,0:T(8,128)(2,1)S(1)}, u32[]{:S(2)}, u32[]{:S(2)}) collective-permute-start(bf16[64,7168]{1,0:T(8,128)(2,1)} %collective-permute-done.7.refs_0_), channel_id=1, source_target_pairs={{2,0},{3,1},{0,2},{1,3},{6,4},{7,5},{4,6},{5,7},{10,8},{11,9},{8,1... | collective-permute-start | bytes 2752520 | tf_op jit(solution)/shard_map/ppermute | solution.py:203
  108.1 42.2 %collective-permute-start.14 = (bf16[64,7168]{1,0:T(8,128)(2,1)}, bf16[64,7168]{1,0:T(8,128)(2,1)}, u32[]{:S(2)}, u32[]{:S(2)}) collective-permute-start(bf16[64,7168]{1,0:T(8,128)(2,1)} %collective-permute-done.13.refs_0_), channel_id=1, source_target_pairs={{2,0},{3,1},{0,2},{1,3},{6,4},{7,5},{4,6},{5,7},{10,8},{11,9},{8,1... | collective-permute-start | bytes 2752520 | tf_op jit(solution)/shard_map/ppermute | solution.py:203
  116.1 52.9 %collective-permute-start.20 = (bf16[64,7168]{1,0:T(8,128)(2,1)}, bf16[64,7168]{1,0:T(8,128)(2,1)}, u32[]{:S(2)}, u32[]{:S(2)}) collective-permute-start(bf16[64,7168]{1,0:T(8,128)(2,1)} %collective-permute-done.19.refs_0_), channel_id=1, source_target_pairs={{2,0},{3,1},{0,2},{1,3},{6,4},{7,5},{4,6},{5,7},{10,8},{11,9},{8,1... | collective-permute-start | bytes 2752520 | tf_op jit(solution)/shard_map/ppermute | solution.py:203
  117.1 51.9 %collective-permute-start.21 = (bf16[64,7168]{1,0:T(8,128)(2,1)}, bf16[64,7168]{1,0:T(8,128)(2,1)}, u32[]{:S(2)}, u32[]{:S(2)}) collective-permute-start(bf16[64,7168]{1,0:T(8,128)(2,1)} %collective-permute-done.19.refs_0_), channel_id=1, source_target_pairs={{0,1},{1,0},{2,3},{3,2},{4,5},{5,4},{6,7},{7,6},{8,9},{9,8},{10,11... | collective-permute-start | bytes 2752520 | tf_op jit(solution)/shard_map/ppermute | solution.py:213
  117.1 17.9 %copy-start = (bf16[4,64,1024]{2,1,0:T(8,128)(2,1)S(1)}, bf16[4,64,1024]{2,1,0:T(8,128)(2,1)}, u32[]{:S(2)}) copy-start(bf16[4,64,1024]{2,1,0:T(8,128)(2,1)} %get-tuple-element.14) | copy-start | bytes 1572868
  133.2 35.7 %copy-start.3 = (bf16[64,7168]{1,0:T(8,128)(2,1)}, bf16[64,7168]{1,0:T(8,128)(2,1)S(1)}, u32[]{:S(2)}) copy-start(bf16[64,7168]{1,0:T(8,128)(2,1)S(1)} %collective-permute-done.8.refs_1_) | copy-start | bytes 2752516
  133.3 36.2 %collective-permute-start.3 = (bf16[128,1024]{1,0:T(8,128)(2,1)S(1)}, bf16[128,1024]{1,0:T(8,128)(2,1)S(1)}, u32[]{:S(2)}, u32[]{:S(2)}) collective-permute-start(bf16[128,1024]{1,0:T(8,128)(2,1)S(1)} %dynamic-slice_bitcast_fusion), channel_id=1, source_target_pairs={{0,4},{4,0},{1,5},{5,1},{2,6},{6,2},{3,7},{7,3},{8,12},{12,8},{9,1... | collective-permute-start | bytes 786440 | tf_op jit(solution)/shard_map/ppermute | solution.py:200
  139.1 30.9 %copy-start.2 = (bf16[128,7168]{1,0:T(8,128)(2,1)S(1)}, bf16[128,7168]{1,0:T(8,128)(2,1)}, u32[]{:S(2)}) copy-start(bf16[128,7168]{1,0:T(8,128)(2,1)} %get-tuple-element.7) | copy-start | bytes 5505028
  150.3 49.2 %collective-permute-start.9 = (bf16[64,7168]{1,0:T(8,128)(2,1)}, bf16[64,7168]{1,0:T(8,128)(2,1)S(1)}, u32[]{:S(2)}, u32[]{:S(2)}) collective-permute-start(bf16[64,7168]{1,0:T(8,128)(2,1)} %collective-permute-done.7.refs_0_), channel_id=1, source_target_pairs={{0,1},{1,0},{2,3},{3,2},{4,5},{5,4},{6,7},{7,6},{8,9},{9,8},{10,11... | collective-permute-start | bytes 2752520 | tf_op jit(solution)/shard_map/ppermute | solution.py:213
  168.9 19.5 %collective-permute-start.15 = (bf16[64,7168]{1,0:T(8,128)(2,1)}, bf16[64,7168]{1,0:T(8,128)(2,1)}, u32[]{:S(2)}, u32[]{:S(2)}) collective-permute-start(bf16[64,7168]{1,0:T(8,128)(2,1)} %collective-permute-done.13.refs_0_), channel_id=1, source_target_pairs={{0,1},{1,0},{2,3},{3,2},{4,5},{5,4},{6,7},{7,6},{8,9},{9,8},{10,11... | collective-permute-start | bytes 2752520 | tf_op jit(solution)/shard_map/ppermute | solution.py:213
  169.0 30.5 %collective-permute-start.10 = (bf16[64,7168]{1,0:T(8,128)(2,1)S(1)}, bf16[64,7168]{1,0:T(8,128)(2,1)}, u32[]{:S(2)}, u32[]{:S(2)}) collective-permute-start(bf16[64,7168]{1,0:T(8,128)(2,1)S(1)} %collective-permute-done.8.refs_1_), channel_id=1, source_target_pairs={{0,1},{1,0},{2,3},{3,2},{4,5},{5,4},{6,7},{7,6},{8,9},{9,8},{10,11... | collective-permute-start | bytes 2752520 | tf_op jit(solution)/shard_map/ppermute | solution.py:213
  169.5 19.0 %collective-permute-start.16 = (bf16[64,7168]{1,0:T(8,128)(2,1)}, bf16[64,7168]{1,0:T(8,128)(2,1)}, u32[]{:S(2)}, u32[]{:S(2)}) collective-permute-start(bf16[64,7168]{1,0:T(8,128)(2,1)} %collective-permute-done.14.refs_1_), channel_id=1, source_target_pairs={{0,1},{1,0},{2,3},{3,2},{4,5},{5,4},{6,7},{7,6},{8,9},{9,8},{10,11... | collective-permute-start | bytes 2752520 | tf_op jit(solution)/shard_map/ppermute | solution.py:213
  169.5 6.0 %collective-permute-start.22 = (bf16[64,7168]{1,0:T(8,128)(2,1)}, bf16[64,7168]{1,0:T(8,128)(2,1)S(1)}, u32[]{:S(2)}, u32[]{:S(2)}) collective-permute-start(bf16[64,7168]{1,0:T(8,128)(2,1)} %collective-permute-done.20.refs_1_), channel_id=1, source_target_pairs={{0,1},{1,0},{2,3},{3,2},{4,5},{5,4},{6,7},{7,6},{8,9},{9,8},{10,11... | collective-permute-start | bytes 2752520 | tf_op jit(solution)/shard_map/ppermute | solution.py:213
  170.0 6.6 %copy-start.1 = (bf16[256,1024]{1,0:T(8,128)(2,1)S(1)}, bf16[256,1024]{1,0:T(8,128)(2,1)}, u32[]{:S(2)}) copy-start(bf16[256,1024]{1,0:T(8,128)(2,1)} %output_partial.1) | copy-start | bytes 1572868
  175.6 1.8 copy-start.5
  175.6 36.4 %collective-permute-start.6 = (bf16[64,7168]{1,0:T(8,128)(2,1)S(1)}, bf16[64,7168]{1,0:T(8,128)(2,1)S(1)}, u32[]{:S(2)}, u32[]{:S(2)}) collective-permute-start(bf16[64,7168]{1,0:T(8,128)(2,1)S(1)} %slice.33), channel_id=1, source_target_pairs={{0,2},{1,3},{2,0},{3,1},{4,6},{5,7},{6,4},{7,5},{8,10},{9,11},{10,... | collective-permute-start | bytes 2752520 | tf_op jit(solution)/shard_map/ppermute | solution.py:208
  199.4 0.9 copy-start.4

commit v2 on v0

v2 whole, which is shorter than its diff:
```python
import functools

import jax
import jax.numpy as jnp
from jax import lax
from jax.experimental import pallas as pl
from jax.experimental.pallas import tpu as pltpu
from jax.sharding import PartitionSpec as P

MIB = 1024 * 1024
COST = pl.CostEstimate(flops=1000, bytes_accessed=1000, transcendentals=0)


def whole(space):
    return pl.BlockSpec(memory_space=space)


def params(mib):
    return pltpu.CompilerParams(vmem_limit_bytes=mib * MIB)


def after(value, *others):
    return lax.optimization_barrier((value, *others))[0]


def tile_of(size, block, most):
    best = block
    for tile in range(block, most + 1, block):
        if size % tile == 0:
            best = tile
    return best


def group_order(n_col):
    col = lax.axis_index("col")
    hi, core, n_hi = col // 2, col % 2, n_col // 2
    near = [((hi + step) % n_hi) * 2 + core for step in range(n_hi)]
    return near + [index + 1 - 2 * core for index in near]


def in_order(parts, natural, n_row):
    row = lax.axis_index("row")
    for step, part in enumerate(parts):
        size = part.shape[0]
        start = pl.multiple_of(((row - step + n_row) % n_row) * size, size)
        natural[pl.ds(start, size), :] = part[...]


def input_kernel(n_row, n_col, slot_of, blocks, *refs):
    parts, refs = refs[:n_row], refs[n_row:]
    sums, (send, dense, natural, grad) = refs[:n_col // 2], refs[n_col // 2:]
    step = pl.program_id(0)
    tile, cols = dense.shape
    block = blocks.shape[1]
    col_blocks = cols // block
    group = sums[0].shape[0]

    @pl.when(step == 0)
    def _():
        in_order(parts, natural, n_row)
        for place, index in enumerate(group_order(n_col)):
            start = pl.multiple_of(index * group, group)
            grad[place * group:(place + 1) * group, :] = natural[pl.ds(start, group), :]

    first = step * (tile // block) * col_blocks

    def row_of_blocks(index, carry):
        top = pl.multiple_of(index * block, block)
        for side in range(col_blocks):
            slot = slot_of[first + index * col_blocks + side]
            values = blocks[jnp.maximum(slot, 0)]
            dense[pl.ds(top, block), side * block:(side + 1) * block] = jnp.where(slot >= 0, values, jnp.zeros_like(values))
        return carry

    lax.fori_loop(0, tile // block, row_of_blocks, 0)
    part = lax.dot_general(grad[...], dense[...], (((1,), (1,)), ((), ())), preferred_element_type=jnp.float32)
    for place, ref in enumerate(sums):
        ref[...] = part[place * group:(place + 1) * group].astype(ref.dtype)
    send[...] = part[n_col // 2 * group:].astype(send.dtype)


def input_partial(n_row, n_col, slot_of, blocks, parts, rows):
    part_rows, cols = parts[0].shape
    tokens = part_rows * n_row
    kind = blocks.dtype
    tile = tile_of(rows, blocks.shape[1], 1792)
    group, n_hi = tokens // n_col, n_col // 2
    shapes = [jax.ShapeDtypeStruct((height, rows), kind) for height in [group] * n_hi + [tokens // 2]]
    specs = [pl.BlockSpec((height, tile), lambda t: (0, t)) for height in [group] * n_hi + [tokens // 2]]
    return pl.pallas_call(
        functools.partial(input_kernel, n_row, n_col),
        grid=(rows // tile,),
        out_shape=(*shapes, jax.ShapeDtypeStruct((rows, cols), kind)),
        in_specs=[whole(pltpu.SMEM)] + [whole(pltpu.VMEM)] * (1 + n_row),
        out_specs=(*specs, pl.BlockSpec((tile, cols), lambda t: (t, 0))),
        scratch_shapes=[pltpu.VMEM((tokens, cols), kind), pltpu.VMEM((tokens, cols), kind)],
        compiler_params=params(44),
        cost_estimate=COST,
        name="input_partial",
    )(slot_of, blocks, *parts)


def output_kernel(n_col, *refs):
    pieces, (dense, out, total) = refs[:n_col], refs[n_col:]
    step = pl.program_id(0)
    group = pieces[0].shape[0]
    hidden = jnp.concatenate([piece[...] for piece in pieces], axis=0)
    part = jnp.dot(hidden, dense[...], preferred_element_type=jnp.float32)

    @pl.when(step == 0)
    def _():
        total[...] = part

    @pl.when(step > 0)
    def _():
        total[...] += part

    @pl.when(step == pl.num_programs(0) - 1)
    def _():
        for place, index in enumerate(group_order(n_col)):
            start = pl.multiple_of(index * group, group)
            out[pl.ds(start, group), :] = total[place * group:(place + 1) * group, :].astype(out.dtype)


def output_partial(n_col, pieces, dense):
    group, rows = pieces[0].shape
    tokens = group * n_col
    cols = dense.shape[1]
    tile = tile_of(rows, 128, 1792)
    return pl.pallas_call(
        functools.partial(output_kernel, n_col),
        grid=(rows // tile,),
        out_shape=jax.ShapeDtypeStruct((tokens, cols), pieces[0].dtype),
        in_specs=[pl.BlockSpec((group, tile), lambda t: (0, t))] * n_col + [pl.BlockSpec((tile, cols), lambda t: (t, 0))],
        out_specs=pl.BlockSpec((tokens, cols), lambda t: (0, 0)),
        scratch_shapes=[pltpu.VMEM((tokens, cols), jnp.float32)],
        compiler_params=params(20),
        cost_estimate=COST,
        name="output_partial",
    )(*pieces, dense)


def weight_kernel(n_dp, n_row, n_col, plan, first, last, scale, kept, *refs):
    count = sum(len(places) for _, places in plan)
    sets = sum(choices for choices, _ in plan) * n_row
    held, refs = refs[:sets], refs[sets:]
    pieces, refs = refs[:count], refs[count:]
    before, refs = (None, refs) if first else (refs[0], refs[1:])
    out, natural, turned = refs
    some_slots, block, _ = out.shape
    group = pieces[0].shape[0]
    col_blocks = turned.shape[0] // block
    order = group_order(n_col)
    dp = lax.axis_index("dp")
    step = pl.program_id(0)
    start_slot = (dp * pl.num_programs(0) + step) * some_slots

    @pl.when(step == 0)
    def _():
        offset, ref = 0, 0
        row = lax.axis_index("row")
        for choices, places in plan:
            for back in range(n_row):
                part = held[ref + back][...]
                if choices == 2:
                    part = jnp.where((dp == 0) | (dp == n_dp - 1), part, held[ref + n_row + back][...])
                size, strips = part.shape[0], part.shape[1] // natural.shape[1]
                for strip in range(strips):
                    start = (((row - back + n_row) % n_row) * strips + strip) * size
                    values = part[:, strip * natural.shape[1]:(strip + 1) * natural.shape[1]]
                    natural[pl.ds(pl.multiple_of(start, size), size), :] = values
            for place in places:
                rows = pl.ds(pl.multiple_of(order[place] * group, group), group)
                turned[:, offset:offset + group] = natural[rows, :].T
                offset += group
            ref += choices * n_row

    at_once = max(size for size in (1, 2, 4, 5, 8) if some_slots % size == 0)

    def some(turn, carry):
        results = []
        for index in range(at_once):
            slot = turn * at_once + index
            chosen = kept[start_slot + slot]
            place = jnp.maximum(chosen, 0)
            top = pl.multiple_of((place // col_blocks) * block, block)
            left = pl.multiple_of((place % col_blocks) * block, block)
            hidden = jnp.concatenate([piece[:, pl.ds(top, block)] for piece in pieces], axis=0)
            part = jnp.dot(turned[pl.ds(left, block), :], hidden, preferred_element_type=jnp.float32)
            if not first:
                part = part + before[slot]
            if last:
                part = jnp.where(chosen >= 0, part * scale, 0.0).T
            results.append(part.astype(out.dtype))
        for index in range(at_once):
            out[turn * at_once + index] = results[index]
        return carry

    lax.fori_loop(0, some_slots // at_once, some, 0)


def weight_partial(sizes, kept, work, before, share, block, cols, scale, last):
    n_dp, n_row, n_col = sizes
    first = before is None
    plan = [(len(entry[0]), entry[1]) for entry in work]
    held = [part for entry in work for parts in entry[0] for part in parts]
    pieces = [piece for entry in work for piece in entry[2]]
    tokens = pieces[0].shape[0] * len(pieces)
    some_slots = share // 5 if share % 5 == 0 else share
    spec = pl.BlockSpec((some_slots, block, block), lambda t: (t, 0, 0))
    extra = [] if first else [before]
    return pl.pallas_call(
        functools.partial(weight_kernel, n_dp, n_row, n_col, plan, first, last, scale),
        grid=(share // some_slots,),
        out_shape=jax.ShapeDtypeStruct((share, block, block), jnp.bfloat16 if last else jnp.float32),
        in_specs=[whole(pltpu.SMEM)] + [whole(pltpu.VMEM)] * (len(held) + len(pieces)) + [spec] * len(extra),
        out_specs=spec,
        scratch_shapes=[
            pltpu.VMEM((n_row * held[0].size // cols, cols), jnp.bfloat16),
            pltpu.VMEM((cols, tokens), jnp.bfloat16),
        ],
        compiler_params=params(20),
        cost_estimate=COST,
        name="weight_partial",
    )(kept, *held, *pieces, *extra)


def on_device(sizes, hidden, weight_blocks, kept_blocks, cotangent):
    n_dp, n_row, n_col = sizes
    block = weight_blocks.shape[-1]
    slots = weight_blocks.shape[2]
    blocks = weight_blocks.reshape(slots, block, block)
    kept = kept_blocks.reshape(slots)
    group, rows = hidden.shape
    part_rows, cols = cotangent.shape
    tokens = group * n_col
    n_hi = n_col // 2
    share = slots // n_dp
    region = (rows // block) * (cols // block)
    dp, row = lax.axis_index("dp"), lax.axis_index("row")

    def shift(value, axis, size, step):
        return lax.ppermute(value, axis, [(index, (index + step) % size) for index in range(size)])

    def from_x(value, step):
        return lax.ppermute(
            value, "col", [(((index // 2 + step) % n_hi) * 2 + index % 2, index) for index in range(n_col)]
        )

    def to_x(value, step):
        return lax.ppermute(
            value, "col", [(index, ((index // 2 + step) % n_hi) * 2 + index % 2) for index in range(n_col)]
        )

    def swap(value):
        return lax.ppermute(value, "col", [(index, index ^ 1) for index in range(n_col)])

    def over_x(value):
        return [from_x(value, step) for step in range(1, n_hi)]

    def all_rows(value):
        return [value] + [shift(value, "row", n_row, step) for step in range(1, n_row)]

    def along(value, pairs):
        return lax.ppermute(value, "dp", pairs)

    every = list(range(n_col))
    call = functools.partial(weight_partial, sizes, kept, share=share, block=block, cols=cols, scale=1.0 / tokens)
    slot_of = jnp.max(
        jnp.where(
            kept[None, :] == jnp.arange(region, dtype=jnp.int32)[:, None], jnp.arange(slots, dtype=jnp.int32)[None, :], -1
        ),
        axis=1,
    )
    line = n_dp == 4 and n_hi == 2 and part_rows % group == 0
    near = [hidden] + over_x(hidden)
    own_parts = all_rows(cotangent)
    if line:
        ends, middle, outward = [(0, 1), (1, 0), (2, 3), (3, 2)], [(1, 2), (2, 1)], [(1, 0), (2, 3)]
        strips = range(0, part_rows, group)
        packed = jnp.concatenate([hidden] + [cotangent[start:start + group] for start in strips], axis=1)
        hop_a, hop_b = along(packed, ends), along(packed, middle)
    *sums, send, dense = input_partial(n_row, n_col, slot_of, blocks, own_parts, rows)

    got = swap(send)
    if line:
        hop_a, hop_b = after(hop_a, send), after(hop_b, send)
        hop_c, hop_d = along(hop_b, outward), along(hop_a, middle)
        swapped = [swap(after(hidden, send, hop_a, hop_b, *near[1:]))]
    else:
        swapped = [swap(hidden)]
    for value in near[1:]:
        swapped.append(swap(after(value, swapped[-1])))
    own = near + swapped
    got = after(got, *own)

    def pair(step):
        return sums[step].astype(jnp.float32) + got[step * group:(step + 1) * group].astype(jnp.float32)

    crossing = [pair(step).astype(jnp.bfloat16) for step in range(1, n_hi)]
    input_grad = pair(0)
    for step, value in enumerate(crossing):
        input_grad = input_grad + to_x(value, step + 1).astype(jnp.float32)
    input_grad = input_grad.astype(jnp.bfloat16)
    part = output_partial(n_col, own, after(dense, *crossing))

    parts = after(part, input_grad).reshape(n_row, part_rows, cols)
    output = lax.dynamic_index_in_dim(parts, row, 0, keepdims=False).astype(jnp.float32)
    for step in range(1, n_row):
        piece = lax.dynamic_index_in_dim(parts, (row + step) % n_row, 0, keepdims=False)
        output = output + shift(piece, "row", n_row, step).astype(jnp.float32)
    output = output.astype(jnp.bfloat16)
    total = call([([[after(own_parts[0], output)] + own_parts[1:]], every, own)], None, last=False)

    if line:
        inner = (dp == 1) | (dp == 2)

        def landed(own_hop, outer_hop):
            return [
                jnp.where(inner, own_hop[:, :rows], outer_hop[:, :rows]),
                jnp.where(inner, own_hop[:, rows:], outer_hop[:, rows:]),
            ]

        hop_c, hop_d = after(hop_c, part), after(hop_d, part)
        hop_e = along(hop_d, outward)
        second, grad_2 = landed(hop_b, hop_c)
        (far_2,) = over_x(after(second, input_grad))
        both = all_rows(after(jnp.concatenate([hop_a[:, rows:], grad_2], axis=0), input_grad))
        rows_1, rows_2 = [value[:group] for value in both], [value[group:] for value in both]

        hop_e = after(hop_e, total)
        third, grad_3 = landed(hop_d, hop_e)
        (far_3,) = over_x(after(third, far_2))
        far_1 = along(after(near[1], hop_e, far_2), ends)
        swap_1, swap_2 = swap(after(hop_a, far_2)), swap(after(second, far_2))
        rows_3 = all_rows(after(grad_3, far_2))
        swap_far_2, swap_3 = swap(after(far_2, swap_1, swap_2)), swap(after(third, swap_1, swap_2))
        work = [
            ([rows_1], [0, 2], [hop_a, swap_1]),
            ([rows_2], every, [second, far_2, swap_2, swap_far_2]),
            ([rows_3], [0, 2], [third, swap_3]),
        ]
        total = call(work, total, last=False)

        far_1, far_3 = after(far_1, total), after(far_3, total)
        work = [([rows_1], [1, 3], [far_1, swap(far_1)]), ([rows_3], [1, 3], [far_3, swap(far_3)])]
        total = call(work, total, last=True)
    else:
        for step in range(1, n_dp):
            piece = shift(hidden, "dp", n_dp, step)
            near = [piece] + over_x(piece)
            held = [all_rows(shift(cotangent, "dp", n_dp, step))]
            total = call([(held, every, near + [swap(value) for value in near])], total, last=step == n_dp - 1)
    return output, input_grad, total.reshape(1, 1, share, block, block)


def solution(mesh):
    in_specs = (
        P(("dp", "col"), "row"),
        P("row", "col", None, None, None),
        P("row", "col", None),
        P(("dp", "row"), "col"),
    )
    out_specs = (
        P(("dp", "row"), "col"),
        P(("dp", "col"), "row"),
        P("row", "col", "dp", None, None),
    )
    sizes = (mesh.shape["dp"], mesh.shape["row"], mesh.shape["col"])
    return jax.shard_map(
        functools.partial(on_device, sizes), mesh=mesh, in_specs=in_specs, out_specs=out_specs, check_vma=False
    )
```

time: 275 us -> 134 us (0.49)
  local copies, waits for them, and re-layouts: 94.7 us -> 9.21 us
  matrix products: 57.9 us -> 0 us
  Pallas kernels: 0 us -> 41.5 us
  other arithmetic: 43.5 us -> 9.8 us
  between operations: 14.2 us -> 0.84 us
  starting transfers between devices: 8.3 us -> 20.6 us
  blocking collectives: 9.98 us -> 0 us
  waiting for transfers between devices: 45.2 us -> 51.1 us
    dot_general x4 -> x0, matrix products: 57.9 us -> none  [the longest x1 22.1 us: on_device(): jnp.einsum('sa,sc,skn->akcn', row_onehot.astype(jnp.bfloat16), col_onehot...]
    ppermute x0 -> x23, waiting for transfers between devices: none -> 51.1 us  [the longest x6 22.2 us: along(): return lax.ppermute(value, 'dp', pairs)]
    pallas_call x0 -> x5, Pallas kernels: none -> 41.5 us  [the longest x3 19.9 us: weight_partial(): pl.pallas_call(functools.partial(weight_kernel, n_dp, n_row, n_col, plan,...]
    unnamed x3 -> x1, other arithmetic: 27.7 us -> 0.02 us
    all_to_all x2 -> x0, waiting for transfers between devices: 26.3 us -> none  [the longest x1 26.3 us: on_device(): lax.all_to_all(input_rounded, 'col', split_axis=1, concat_axis=0, tiled=T...]
    gather x2 -> x0, local copies, waits for them, and re-layouts: 24.6 us -> none  [the longest x1 13.4 us: on_device(): jnp.take(gathered_hidden.reshape(tokens_all, row_blocks, block_size), blo...]
    reshape x4 -> x0, local copies, waits for them, and re-layouts: 23.6 us -> none  [the longest x1 16.4 us: on_device(): input_rounded = input_part.astype(jnp.bfloat16).reshape(1, tokens_all, -1)]
    ppermute x0 -> x23, starting transfers between devices: none -> 20.6 us  [the longest x6 8.51 us: along(): return lax.ppermute(value, 'dp', pairs)]
  transfers between devices with their start and end apart: 4 -> 23, of which waited for: 3 -> 14; matrix products, arithmetic and copies ran while one was open for 53% -> 6% of each run, Pallas kernels for 0% -> 26%
where the time goes in v2:
time: 134 us; the launch traced here: 133 us
  waiting for transfers between devices  51.1 us (38%)
  Pallas kernels  41.5 us (31%)
  starting transfers between devices  20.6 us (15%)
  other arithmetic  9.8 us (7%)
  local copies, waits for them, and re-layouts  9.21 us (7%)
    ppermute x6, waiting for transfers between devices, along(): return lax.ppermute(value, 'dp', pairs)  22.2 us
    pallas_call x3, Pallas kernels, weight_partial(): pl.pallas_call(functools.partial(weight_kernel, n_dp, n_row, n_col, plan,...  19.9 us
    ppermute x4, waiting for transfers between devices, shift(): lax.ppermute(value, axis, [(index, (index + step) % size) for index in ra...  19.7 us
    pallas_call x1, Pallas kernels, input_partial(): pl.pallas_call(functools.partial(input_kernel, n_row, n_col), grid=(rows...  15.5 us
    ppermute x6, starting transfers between devices, along(): return lax.ppermute(value, 'dp', pairs)  8.51 us
    ppermute x9, waiting for transfers between devices, swap(): lax.ppermute(value, 'col', [(index, index ^ 1) for index in range(n_col)])  7.29 us
    unnamed x14, local copies, waits for them, and re-layouts  7.06 us
    pallas_call x1, Pallas kernels, output_partial(): pl.pallas_call(functools.partial(output_kernel, n_col), grid=(rows // til...  6.02 us
  transfers between devices with their start and end apart: 23, of which 14 were waited for; matrix products, arithmetic and copies ran while one was open for 6% of the time, Pallas kernels for 26%

profile of v2, /device:TPU:0, one launch (start us, length us, event | category | flops | bytes accessed | tf_op | source)
XLA Modules:
  0.0 133.0 jit_solution(16039167484803211004)
XLA Ops:
  0.6 0.0 copy-start.1
  0.7 1.1 fusion.3
  1.7 2.3 %pad_maximum_fusion = bf16[64,9216]{1,0:T(8,128)(2,1)} fusion(bf16[64,1024]{1,0:T(8,128)(2,1)S(1)} %get-tuple-element.60, bf16[64,1024]{1,0:T(8,128)(2,1)S(1)} %get-tuple-element.59, bf16[64,7168]{1,0:T(8,128)(2,1)} %refs_2_.1), kind=kLoop, calls=%fused_computation.2 | loop fusion | flops 3538944 | bytes 2359296 | tf_op jit(solution)/shard_map/concatenate | solution.py:281
  4.0 3.0 %collective-permute-start.2 = (bf16[64,9216]{1,0:T(8,128)(2,1)}, bf16[64,9216]{1,0:T(8,128)(2,1)}, u32[]{:S(2)}, u32[]{:S(2)}) collective-permute-start(bf16[64,9216]{1,0:T(8,128)(2,1)} %pad_maximum_fusion), channel_id=1, source_target_pairs={{0,8},{8,0},{16,24},{24,16},{1,9},{9,1},{17,25},{25,17},{2,10},{10... | collective-permute-start | bytes 3538952 | tf_op jit(solution)/shard_map/ppermute | solution.py:265
  7.1 1.7 %collective-permute-start.3 = (bf16[64,9216]{1,0:T(8,128)(2,1)}, bf16[64,9216]{1,0:T(8,128)(2,1)}, u32[]{:S(2)}, u32[]{:S(2)}) collective-permute-start(bf16[64,9216]{1,0:T(8,128)(2,1)} %pad_maximum_fusion), channel_id=1, source_target_pairs={{8,16},{16,8},{9,17},{17,9},{10,18},{18,10},{11,19},{19,11},{12,20... | collective-permute-start | bytes 3538952 | tf_op jit(solution)/shard_map/ppermute | solution.py:265
  8.8 1.5 %collective-permute-start = (bf16[64,7168]{1,0:T(8,128)(2,1)S(1)}, bf16[64,7168]{1,0:T(8,128)(2,1)S(1)}, u32[]{:S(2)}, u32[]{:S(2)}) collective-permute-start(bf16[64,7168]{1,0:T(8,128)(2,1)S(1)} %copy-done.1), channel_id=1, source_target_pairs={{2,0},{3,1},{0,2},{1,3},{6,4},{7,5},{4,6},{5,7},{10,8},{11,9},{8,1... | collective-permute-start | bytes 2752520 | tf_op jit(solution)/shard_map/ppermute | solution.py:246
  10.2 1.5 %collective-permute-start.1 = (bf16[128,1024]{1,0:T(8,128)(2,1)S(1)}, bf16[128,1024]{1,0:T(8,128)(2,1)S(1)}, u32[]{:S(2)}, u32[]{:S(2)}) collective-permute-start(bf16[128,1024]{1,0:T(8,128)(2,1)S(1)} %copy-done.2), channel_id=1, source_target_pairs={{0,4},{4,0},{1,5},{5,1},{2,6},{6,2},{3,7},{7,3},{8,12},{12,8},{9,1... | collective-permute-start | bytes 786440 | tf_op jit(solution)/shard_map/ppermute | solution.py:243
  11.8 0.2 select_reduce_fusion.slot_of
  12.0 5.8 %collective-permute-done.1.refs_1_ = bf16[128,1024]{1,0:T(8,128)(2,1)S(1)} collective-permute-done((bf16[128,1024]{1,0:T(8,128)(2,1)S(1)}, bf16[128,1024]{1,0:T(8,128)(2,1)S(1)}, u32[]{:S(2)}, u32[]{:S(2)}) %collective-permute-start.1) | collective-permute-done | bytes 262176 | tf_op jit(solution)/shard_map/ppermute | solution.py:243
  17.7 15.5 %input_partial.1 = (bf16[64,7168]{1,0:T(8,128)(2,1)S(1)}, bf16[64,7168]{1,0:T(8,128)(2,1)S(1)}, bf16[128,7168]{1,0:T(8,128)(2,1)}, bf16[7168,1024]{1,0:T(8,128)(2,1)}) custom-call(s32[448]{0:T(512)S(1)} %select_reduce_fusion.slot_of, bf16[320,128,128]{2,1,0:T(8,128)(2,1)} %bitcast.10, bf16[128,1024]{1,0:T(8,128)(2,1)S(1)} %copy-done.2, ...), custom_call_target="tpu_custom_call" | custom-call | flops 1000 | bytes 1000 | tf_op jit(solution)/shard_map/input_partial/pallas_call | solution.py:90
  33.3 0.9 copy-done.3
  34.2 0.9 copy-done.5
  35.1 0.0 collective-permute-done.2.refs_6_
  35.1 0.0 collective-permute-done.3
  35.1 0.0 collective-permute-done.refs_1_.refs_3_
  35.1 0.1 collective-permute-start.4
  35.2 0.5 collective-permute-start.6
  35.7 2.5 %collective-permute-done.4.refs_2_.refs_4_ = bf16[64,7168]{1,0:T(8,128)(2,1)S(1)} collective-permute-done((bf16[64,7168]{1,0:T(8,128)(2,1)S(1)}, bf16[64,7168]{1,0:T(8,128)(2,1)S(1)}, u32[]{:S(2)}, u32[]{:S(2)}) %collective-permute-start.4) | collective-permute-done | bytes 917536 | tf_op jit(solution)/shard_map/ppermute | solution.py:256
  38.2 0.1 collective-permute-start.5
  38.3 0.7 collective-permute-start.11
  39.1 1.3 collective-permute-start.9
  40.4 1.0 slice.55
  41.4 0.0 collective-permute-done.6
  41.4 0.4 collective-permute-done.5.refs_3_.refs_5_
  41.8 1.7 %add_convert_fusion.1 = bf16[64,7168]{1,0:T(8,128)(2,1)S(1)} fusion(bf16[64,7168]{1,0:T(8,128)(2,1)} %copy-done.5, bf16[128,7168]{1,0:T(8,128)(2,1)} %collective-permute-done.6), kind=kLoop, calls=%fused_computation.1 | loop fusion | flops 1835008 | bytes 2752512 | tf_op jit(solution)/shard_map/convert_element_type | solution.py:300
  43.4 0.6 collective-permute-start.7
  44.0 5.2 %copy-done = bf16[7168,1024]{1,0:T(8,128)(2,1)S(1)} copy-done((bf16[7168,1024]{1,0:T(8,128)(2,1)S(1)}, bf16[7168,1024]{1,0:T(8,128)(2,1)}, u32[]{:S(2)}) %copy-start) | copy-done | bytes 14680088
  49.2 6.0 %output_partial.1 = bf16[256,1024]{1,0:T(8,128)(2,1)S(1)} custom-call(bf16[64,7168]{1,0:T(8,128)(2,1)S(1)} %copy-done.1, bf16[64,7168]{1,0:T(8,128)(2,1)S(1)} %collective-permute-done.refs_1_.refs_3_, bf16[64,7168]{1,0:T(8,128)(2,1)S(1)} %collective-permute-done.4.refs_2_.refs_4_, bf16[64,7168]{1,0:T(8,128)(2,1)} %collective-permute-done.5.refs_3_.refs_5_, ...), custom_call_target="tpu_custom_call" | custom-call | flops 1000 | bytes 1000 | tf_op jit(solution)/shard_map/output_partial/pallas_call | solution.py:130
  55.2 0.0 collective-permute-done.11
  55.3 1.4 %collective-permute-start.12 = (bf16[64,9216]{1,0:T(8,128)(2,1)S(1)}, bf16[64,9216]{1,0:T(8,128)(2,1)S(1)}, u32[]{:S(2)}, u32[]{:S(2)}) collective-permute-start(bf16[64,9216]{1,0:T(8,128)(2,1)S(1)} %collective-permute-done.11), channel_id=1, source_target_pairs={{8,0},{16,24},{9,1},{17,25},{10,2},{18,26},{11,3},{19,27},{12,4},{... | collective-permute-start | bytes 3538952 | tf_op jit(solution)/shard_map/ppermute | solution.py:265
  56.7 16.7 %collective-permute-done.9 = bf16[64,9216]{1,0:T(8,128)(2,1)S(1)} collective-permute-done((bf16[64,9216]{1,0:T(8,128)(2,1)}, bf16[64,9216]{1,0:T(8,128)(2,1)S(1)}, u32[]{:S(2)}, u32[]{:S(2)}) %collective-permute-start.9) | collective-permute-done | bytes 1179680 | tf_op jit(solution)/shard_map/ppermute | solution.py:265
  73.4 1.3 slice_select_fusion.1.refs_8_
  74.6 1.0 slice_select_fusion.3
  75.6 0.0 collective-permute-done.7
  75.6 2.4 %add_convert_fusion = bf16[64,7168]{1,0:T(8,128)(2,1)} fusion(bf16[64,7168]{1,0:T(8,128)(2,1)S(1)} %collective-permute-done.7, bf16[64,7168]{1,0:T(8,128)(2,1)S(1)} %copy-done.4, bf16[128,7168]{1,0:T(8,128)(2,1)} %collective-permute-done.6), kind=kLoop, calls=%fused_computation | loop fusion | flops 2752512 | bytes 3670016 | tf_op jit(solution)/shard_map/convert_element_type | solution.py:304
  78.1 1.5 %collective-permute-start.13 = (bf16[64,7168]{1,0:T(8,128)(2,1)S(1)}, bf16[64,7168]{1,0:T(8,128)(2,1)S(1)}, u32[]{:S(2)}, u32[]{:S(2)}) collective-permute-start(bf16[64,7168]{1,0:T(8,128)(2,1)S(1)} %slice_select_fusion.1.refs_8_), channel_id=1, source_target_pairs={{2,0},{3,1},{0,2},{1,3},{6,4},{7,5},{4,6},{5,7},{10,8},{11,9},{8,1... | collective-permute-start | bytes 2752520 | tf_op jit(solution)/shard_map/ppermute | solution.py:246
  79.7 1.6 %collective-permute-start.8 = (bf16[128,1024]{1,0:T(8,128)(2,1)S(1)}, bf16[128,1024]{1,0:T(8,128)(2,1)S(1)}, u32[]{:S(2)}, u32[]{:S(2)}) collective-permute-start(bf16[128,1024]{1,0:T(8,128)(2,1)S(1)} %dynamic-slice_bitcast_fusion), channel_id=1, source_target_pairs={{0,4},{4,0},{1,5},{5,1},{2,6},{6,2},{3,7},{7,3},{8,12},{12,8},{9,1... | collective-permute-start | bytes 786440 | tf_op jit(solution)/shard_map/ppermute | solution.py:243
  81.2 0.5 collective-permute-start.10
  81.8 7.2 %collective-permute-done.8 = bf16[128,1024]{1,0:T(8,128)(2,1)S(1)} collective-permute-done((bf16[128,1024]{1,0:T(8,128)(2,1)S(1)}, bf16[128,1024]{1,0:T(8,128)(2,1)S(1)}, u32[]{:S(2)}, u32[]{:S(2)}) %collective-permute-start.8) | collective-permute-done | bytes 262176 | tf_op jit(solution)/shard_map/ppermute | solution.py:243
  89.0 0.8 fusion
  89.7 5.5 %weight_partial.3.refs_14_ = f32[80,128,128]{2,1,0:T(8,128)S(1)} custom-call(s32[320]{0:T(512)S(1)} %reduce.kept, bf16[128,1024]{1,0:T(8,128)(2,1)S(1)} %copy-done.2, bf16[128,1024]{1,0:T(8,128)(2,1)S(1)} %collective-permute-done.1.refs_1_, bf16[64,7168]{1,0:T(8,128)(2,1)S(1)} %copy-done.1, bf16[64,7168]{1,0:T(8,128)(2,1)S(1)} %collective-permute-done.refs_1_.refs_3_, ...), custom_call_target="tpu_custom_call" | custom-call | flops 1000 | bytes 1000 | tf_op jit(solution)/shard_map/weight_partial/pallas_call | solution.py:212
  95.2 4.3 %collective-permute-done.12 = bf16[64,9216]{1,0:T(8,128)(2,1)S(1)} collective-permute-done((bf16[64,9216]{1,0:T(8,128)(2,1)S(1)}, bf16[64,9216]{1,0:T(8,128)(2,1)S(1)}, u32[]{:S(2)}, u32[]{:S(2)}) %collective-permute-start.12) | collective-permute-done | bytes 1179680 | tf_op jit(solution)/shard_map/ppermute | solution.py:265
  99.5 0.4 collective-permute-done.13.refs_9_
  99.9 0.0 collective-permute-start.17
  99.9 0.5 collective-permute-start.16
  100.4 0.1 slice_select_fusion.refs_12_
  100.5 1.6 %collective-permute-start.21 = (bf16[64,7168]{1,0:T(8,128)(2,1)S(1)}, bf16[64,7168]{1,0:T(8,128)(2,1)S(1)}, u32[]{:S(2)}, u32[]{:S(2)}) collective-permute-start(bf16[64,7168]{1,0:T(8,128)(2,1)S(1)} %slice_select_fusion.refs_12_), channel_id=1, source_target_pairs={{2,0},{3,1},{0,2},{1,3},{6,4},{7,5},{4,6},{5,7},{10,8},{11,9},{8,1... | collective-permute-start | bytes 2752520 | tf_op jit(solution)/shard_map/ppermute | solution.py:246
  102.1 0.4 collective-permute-start.15
  102.4 1.2 collective-permute-done.17.refs_10_
  103.6 0.6 collective-permute-done.16.refs_7_
  104.3 0.1 collective-permute-start.19
  104.4 0.4 collective-permute-start.18
  104.8 0.0 collective-permute-done.10
  104.8 1.6 %collective-permute-start.14 = (bf16[64,2048]{1,0:T(8,128)(2,1)S(1)}, bf16[64,2048]{1,0:T(8,128)(2,1)S(1)}, u32[]{:S(2)}, u32[]{:S(2)}) collective-permute-start(bf16[64,2048]{1,0:T(8,128)(2,1)S(1)} %slice_select_fusion.2.refs_4_.refs_2_), channel_id=1, source_target_pairs={{0,4},{4,0},{1,5},{5,1},{2,6},{6,2},{3,7},{7,3},{8,12},{12,8},{9,1... | collective-permute-start | bytes 786440 | tf_op jit(solution)/shard_map/ppermute | solution.py:243
  106.5 6.8 %collective-permute-done.14.refs_5_.refs_3_ = bf16[64,2048]{1,0:T(8,128)(2,1)S(1)} collective-permute-done((bf16[64,2048]{1,0:T(8,128)(2,1)S(1)}, bf16[64,2048]{1,0:T(8,128)(2,1)S(1)}, u32[]{:S(2)}, u32[]{:S(2)}) %collective-permute-start.14) | collective-permute-done | bytes 262176 | tf_op jit(solution)/shard_map/ppermute | solution.py:243
  113.2 0.0 collective-permute-done.19.refs_13_
  113.2 0.0 collective-permute-done.18.refs_11_
  113.2 8.0 %weight_partial.4.refs_8_ = f32[80,128,128]{2,1,0:T(8,128)S(1)} custom-call(s32[320]{0:T(512)S(1)} %reduce.kept, bf16[64,2048]{1,0:T(8,128)(2,1)S(1)} %get-tuple-element.58.refs_0_, bf16[64,2048]{1,0:T(8,128)(2,1)S(1)} %get-tuple-element.56.refs_1_, bf16[64,2048]{1,0:T(8,128)(2,1)S(1)} %get-tuple-element.57.refs_2_, ...), custom_call_target="tpu_custom_call" | custom-call | flops 1000 | bytes 1000 | tf_op jit(solution)/shard_map/weight_partial/pallas_call | solution.py:212
  121.3 1.6 %collective-permute-done.21.refs_6_ = bf16[64,7168]{1,0:T(8,128)(2,1)S(1)} collective-permute-done((bf16[64,7168]{1,0:T(8,128)(2,1)S(1)}, bf16[64,7168]{1,0:T(8,128)(2,1)S(1)}, u32[]{:S(2)}, u32[]{:S(2)}) %collective-permute-start.21) | collective-permute-done | bytes 917536 | tf_op jit(solution)/shard_map/ppermute | solution.py:246
  122.8 0.0 collective-permute-start.22
  122.8 1.2 collective-permute-done.15.refs_4_
  124.0 1.3 collective-permute-done.22.refs_7_
  125.3 1.3 collective-permute-done.20.refs_5_
  126.6 6.4 %weight_partial.5 = bf16[80,128,128]{2,1,0:T(8,128)(2,1)} custom-call(s32[320]{0:T(512)S(1)} %reduce.kept, bf16[64,2048]{1,0:T(8,128)(2,1)S(1)} %get-tuple-element.58.refs_0_, bf16[64,2048]{1,0:T(8,128)(2,1)S(1)} %get-tuple-element.56.refs_1_, bf16[64,2048]{1,0:T(8,128)(2,1)S(1)} %slice_select_fusion.2.refs_4_.refs_2_, ...), custom_call_target="tpu_custom_call" | custom-call | flops 1000 | bytes 1000 | tf_op jit(solution)/shard_map/weight_partial/pallas_call | solution.py:212
  (17 shorter events, 0.2 us)
Async XLA Ops:
  0.6 9.6 %copy-start.2 = (bf16[128,1024]{1,0:T(8,128)(2,1)S(1)}, bf16[128,1024]{1,0:T(8,128)(2,1)}, u32[]{:S(2)}) copy-start(bf16[128,1024]{1,0:T(8,128)(2,1)} %refs_0_.4) | copy-start | bytes 786436
  0.6 8.1 %copy-start.1 = (bf16[64,7168]{1,0:T(8,128)(2,1)S(1)}, bf16[64,7168]{1,0:T(8,128)(2,1)}, u32[]{:S(2)}) copy-start(bf16[64,7168]{1,0:T(8,128)(2,1)} %refs_2_.1) | copy-start | bytes 2752516
  0.7 11.1 %copy-start.6 = (s32[1,1,320]{2,1,0:T(1,128)S(1)}, s32[1,1,320]{2,1,0:T(1,128)}, u32[]{:S(2)}) copy-start(s32[1,1,320]{2,1,0:T(1,128)} %param.6) | copy-start | bytes 3844
  4.0 31.1 %collective-permute-start.2 = (bf16[64,9216]{1,0:T(8,128)(2,1)}, bf16[64,9216]{1,0:T(8,128)(2,1)}, u32[]{:S(2)}, u32[]{:S(2)}) collective-permute-start(bf16[64,9216]{1,0:T(8,128)(2,1)} %pad_maximum_fusion), channel_id=1, source_target_pairs={{0,8},{8,0},{16,24},{24,16},{1,9},{9,1},{17,25},{25,17},{2,10},{10... | collective-permute-start | bytes 3538952 | tf_op jit(solution)/shard_map/ppermute | solution.py:265
  7.1 28.1 %collective-permute-start.3 = (bf16[64,9216]{1,0:T(8,128)(2,1)}, bf16[64,9216]{1,0:T(8,128)(2,1)}, u32[]{:S(2)}, u32[]{:S(2)}) collective-permute-start(bf16[64,9216]{1,0:T(8,128)(2,1)} %pad_maximum_fusion), channel_id=1, source_target_pairs={{8,16},{16,8},{9,17},{17,9},{10,18},{18,10},{11,19},{19,11},{12,20... | collective-permute-start | bytes 3538952 | tf_op jit(solution)/shard_map/ppermute | solution.py:265
  8.8 26.4 %collective-permute-start = (bf16[64,7168]{1,0:T(8,128)(2,1)S(1)}, bf16[64,7168]{1,0:T(8,128)(2,1)S(1)}, u32[]{:S(2)}, u32[]{:S(2)}) collective-permute-start(bf16[64,7168]{1,0:T(8,128)(2,1)S(1)} %copy-done.1), channel_id=1, source_target_pairs={{2,0},{3,1},{0,2},{1,3},{6,4},{7,5},{4,6},{5,7},{10,8},{11,9},{8,1... | collective-permute-start | bytes 2752520 | tf_op jit(solution)/shard_map/ppermute | solution.py:246
  10.2 7.5 %collective-permute-start.1 = (bf16[128,1024]{1,0:T(8,128)(2,1)S(1)}, bf16[128,1024]{1,0:T(8,128)(2,1)S(1)}, u32[]{:S(2)}, u32[]{:S(2)}) collective-permute-start(bf16[128,1024]{1,0:T(8,128)(2,1)S(1)} %copy-done.2), channel_id=1, source_target_pairs={{0,4},{4,0},{1,5},{5,1},{2,6},{6,2},{3,7},{7,3},{8,12},{12,8},{9,1... | collective-permute-start | bytes 786440 | tf_op jit(solution)/shard_map/ppermute | solution.py:243
  33.3 0.9 copy-start.3
  34.2 0.9 copy-start.5
  35.1 3.1 %collective-permute-start.4 = (bf16[64,7168]{1,0:T(8,128)(2,1)S(1)}, bf16[64,7168]{1,0:T(8,128)(2,1)S(1)}, u32[]{:S(2)}, u32[]{:S(2)}) collective-permute-start(bf16[64,7168]{1,0:T(8,128)(2,1)S(1)} %copy-done.1), channel_id=1, source_target_pairs={{0,1},{1,0},{2,3},{3,2},{4,5},{5,4},{6,7},{7,6},{8,9},{9,8},{10,11... | collective-permute-start | bytes 2752520 | tf_op jit(solution)/shard_map/ppermute | solution.py:256
  35.2 6.1 %collective-permute-start.6 = (bf16[128,7168]{1,0:T(8,128)(2,1)}, bf16[128,7168]{1,0:T(8,128)(2,1)}, u32[]{:S(2)}, u32[]{:S(2)}) collective-permute-start(bf16[128,7168]{1,0:T(8,128)(2,1)} %get-tuple-element.29), channel_id=1, source_target_pairs={{0,1},{1,0},{2,3},{3,2},{4,5},{5,4},{6,7},{7,6},{8,9},{9,8},{10,11... | collective-permute-start | bytes 5505032 | tf_op jit(solution)/shard_map/ppermute | solution.py:256
  38.2 3.5 %collective-permute-start.5 = (bf16[64,7168]{1,0:T(8,128)(2,1)S(1)}, bf16[64,7168]{1,0:T(8,128)(2,1)}, u32[]{:S(2)}, u32[]{:S(2)}) collective-permute-start(bf16[64,7168]{1,0:T(8,128)(2,1)S(1)} %collective-permute-done.refs_1_.refs_3_), channel_id=1, source_target_pairs={{0,1},{1,0},{2,3},{3,2},{4,5},{5,4},{6,7},{7,6},{8,9},{9,8},{10,11... | collective-permute-start | bytes 2752520 | tf_op jit(solution)/shard_map/ppermute | solution.py:256
  38.3 16.9 %collective-permute-start.11 = (bf16[64,9216]{1,0:T(8,128)(2,1)}, bf16[64,9216]{1,0:T(8,128)(2,1)S(1)}, u32[]{:S(2)}, u32[]{:S(2)}) collective-permute-start(bf16[64,9216]{1,0:T(8,128)(2,1)} %collective-permute-done.2.refs_6_), channel_id=1, source_target_pairs={{8,16},{16,8},{9,17},{17,9},{10,18},{18,10},{11,19},{19,11},{12,20... | collective-permute-start | bytes 3538952 | tf_op jit(solution)/shard_map/ppermute | solution.py:265
  39.1 34.3 %collective-permute-start.9 = (bf16[64,9216]{1,0:T(8,128)(2,1)}, bf16[64,9216]{1,0:T(8,128)(2,1)S(1)}, u32[]{:S(2)}, u32[]{:S(2)}) collective-permute-start(bf16[64,9216]{1,0:T(8,128)(2,1)} %collective-permute-done.3), channel_id=1, source_target_pairs={{8,0},{16,24},{9,1},{17,25},{10,2},{18,26},{11,3},{19,27},{12,4},{... | collective-permute-start | bytes 3538952 | tf_op jit(solution)/shard_map/ppermute | solution.py:265
  43.4 32.2 %collective-permute-start.7 = (bf16[64,7168]{1,0:T(8,128)(2,1)S(1)}, bf16[64,7168]{1,0:T(8,128)(2,1)S(1)}, u32[]{:S(2)}, u32[]{:S(2)}) collective-permute-start(bf16[64,7168]{1,0:T(8,128)(2,1)S(1)} %add_convert_fusion.1), channel_id=1, source_target_pairs={{0,2},{1,3},{2,0},{3,1},{4,6},{5,7},{6,4},{7,5},{8,10},{9,11},{10,... | collective-permute-start | bytes 2752520 | tf_op jit(solution)/shard_map/ppermute | solution.py:251
  44.0 5.2 %copy-start = (bf16[7168,1024]{1,0:T(8,128)(2,1)S(1)}, bf16[7168,1024]{1,0:T(8,128)(2,1)}, u32[]{:S(2)}) copy-start(bf16[7168,1024]{1,0:T(8,128)(2,1)} %get-tuple-element.37.refs_4_) | copy-start | bytes 44040196
  55.2 20.4 %copy-start.4 = (bf16[64,7168]{1,0:T(8,128)(2,1)S(1)}, bf16[64,7168]{1,0:T(8,128)(2,1)}, u32[]{:S(2)}) copy-start(bf16[64,7168]{1,0:T(8,128)(2,1)} %copy-done.3) | copy-start | bytes 2752516
  55.3 44.3 %collective-permute-start.12 = (bf16[64,9216]{1,0:T(8,128)(2,1)S(1)}, bf16[64,9216]{1,0:T(8,128)(2,1)S(1)}, u32[]{:S(2)}, u32[]{:S(2)}) collective-permute-start(bf16[64,9216]{1,0:T(8,128)(2,1)S(1)} %collective-permute-done.11), channel_id=1, source_target_pairs={{8,0},{16,24},{9,1},{17,25},{10,2},{18,26},{11,3},{19,27},{12,4},{... | collective-permute-start | bytes 3538952 | tf_op jit(solution)/shard_map/ppermute | solution.py:265
  78.1 21.8 %collective-permute-start.13 = (bf16[64,7168]{1,0:T(8,128)(2,1)S(1)}, bf16[64,7168]{1,0:T(8,128)(2,1)S(1)}, u32[]{:S(2)}, u32[]{:S(2)}) collective-permute-start(bf16[64,7168]{1,0:T(8,128)(2,1)S(1)} %slice_select_fusion.1.refs_8_), channel_id=1, source_target_pairs={{2,0},{3,1},{0,2},{1,3},{6,4},{7,5},{4,6},{5,7},{10,8},{11,9},{8,1... | collective-permute-start | bytes 2752520 | tf_op jit(solution)/shard_map/ppermute | solution.py:246
  79.7 9.3 %collective-permute-start.8 = (bf16[128,1024]{1,0:T(8,128)(2,1)S(1)}, bf16[128,1024]{1,0:T(8,128)(2,1)S(1)}, u32[]{:S(2)}, u32[]{:S(2)}) collective-permute-start(bf16[128,1024]{1,0:T(8,128)(2,1)S(1)} %dynamic-slice_bitcast_fusion), channel_id=1, source_target_pairs={{0,4},{4,0},{1,5},{5,1},{2,6},{6,2},{3,7},{7,3},{8,12},{12,8},{9,1... | collective-permute-start | bytes 786440 | tf_op jit(solution)/shard_map/ppermute | solution.py:243
  81.2 23.6 %collective-permute-start.10 = (bf16[128,2048]{1,0:T(8,128)(2,1)S(1)}, bf16[128,2048]{1,0:T(8,128)(2,1)S(1)}, u32[]{:S(2)}, u32[]{:S(2)}) collective-permute-start(bf16[128,2048]{1,0:T(8,128)(2,1)S(1)} %pad_maximum_fusion.1), channel_id=1, source_target_pairs={{0,4},{4,0},{1,5},{5,1},{2,6},{6,2},{3,7},{7,3},{8,12},{12,8},{9,1... | collective-permute-start | bytes 1572872 | tf_op jit(solution)/shard_map/ppermute | solution.py:243
  99.9 3.7 %collective-permute-start.17 = (bf16[64,7168]{1,0:T(8,128)(2,1)S(1)}, bf16[64,7168]{1,0:T(8,128)(2,1)S(1)}, u32[]{:S(2)}, u32[]{:S(2)}) collective-permute-start(bf16[64,7168]{1,0:T(8,128)(2,1)S(1)} %slice_select_fusion.1.refs_8_), channel_id=1, source_target_pairs={{0,1},{1,0},{2,3},{3,2},{4,5},{5,4},{6,7},{7,6},{8,9},{9,8},{10,11... | collective-permute-start | bytes 2752520 | tf_op jit(solution)/shard_map/ppermute | solution.py:256
  99.9 4.4 %collective-permute-start.16 = (bf16[64,9216]{1,0:T(8,128)(2,1)}, bf16[64,9216]{1,0:T(8,128)(2,1)S(1)}, u32[]{:S(2)}, u32[]{:S(2)}) collective-permute-start(bf16[64,9216]{1,0:T(8,128)(2,1)} %collective-permute-done.2.refs_6_), channel_id=1, source_target_pairs={{0,1},{1,0},{2,3},{3,2},{4,5},{5,4},{6,7},{7,6},{8,9},{9,8},{10,11... | collective-permute-start | bytes 3538952 | tf_op jit(solution)/shard_map/ppermute | solution.py:256
  100.5 22.3 %collective-permute-start.21 = (bf16[64,7168]{1,0:T(8,128)(2,1)S(1)}, bf16[64,7168]{1,0:T(8,128)(2,1)S(1)}, u32[]{:S(2)}, u32[]{:S(2)}) collective-permute-start(bf16[64,7168]{1,0:T(8,128)(2,1)S(1)} %slice_select_fusion.refs_12_), channel_id=1, source_target_pairs={{2,0},{3,1},{0,2},{1,3},{6,4},{7,5},{4,6},{5,7},{10,8},{11,9},{8,1... | collective-permute-start | bytes 2752520 | tf_op jit(solution)/shard_map/ppermute | solution.py:246
  102.1 22.0 %collective-permute-start.15 = (bf16[64,7168]{1,0:T(8,128)(2,1)S(1)}, bf16[64,7168]{1,0:T(8,128)(2,1)S(1)}, u32[]{:S(2)}, u32[]{:S(2)}) collective-permute-start(bf16[64,7168]{1,0:T(8,128)(2,1)S(1)} %collective-permute-done.refs_1_.refs_3_), channel_id=1, source_target_pairs={{0,8},{8,0},{16,24},{24,16},{1,9},{9,1},{17,25},{25,17},{2,10},{10... | collective-permute-start | bytes 2752520 | tf_op jit(solution)/shard_map/ppermute | solution.py:265
  104.3 9.0 %collective-permute-start.19 = (bf16[64,7168]{1,0:T(8,128)(2,1)S(1)}, bf16[64,7168]{1,0:T(8,128)(2,1)S(1)}, u32[]{:S(2)}, u32[]{:S(2)}) collective-permute-start(bf16[64,7168]{1,0:T(8,128)(2,1)S(1)} %slice_select_fusion.refs_12_), channel_id=1, source_target_pairs={{0,1},{1,0},{2,3},{3,2},{4,5},{5,4},{6,7},{7,6},{8,9},{9,8},{10,11... | collective-permute-start | bytes 2752520 | tf_op jit(solution)/shard_map/ppermute | solution.py:256
  104.4 8.8 %collective-permute-start.18 = (bf16[64,7168]{1,0:T(8,128)(2,1)S(1)}, bf16[64,7168]{1,0:T(8,128)(2,1)S(1)}, u32[]{:S(2)}, u32[]{:S(2)}) collective-permute-start(bf16[64,7168]{1,0:T(8,128)(2,1)S(1)} %collective-permute-done.13.refs_9_), channel_id=1, source_target_pairs={{0,1},{1,0},{2,3},{3,2},{4,5},{5,4},{6,7},{7,6},{8,9},{9,8},{10,11... | collective-permute-start | bytes 2752520 | tf_op jit(solution)/shard_map/ppermute | solution.py:256
  104.8 8.4 %collective-permute-start.14 = (bf16[64,2048]{1,0:T(8,128)(2,1)S(1)}, bf16[64,2048]{1,0:T(8,128)(2,1)S(1)}, u32[]{:S(2)}, u32[]{:S(2)}) collective-permute-start(bf16[64,2048]{1,0:T(8,128)(2,1)S(1)} %slice_select_fusion.2.refs_4_.refs_2_), channel_id=1, source_target_pairs={{0,4},{4,0},{1,5},{5,1},{2,6},{6,2},{3,7},{7,3},{8,12},{12,8},{9,1... | collective-permute-start | bytes 786440 | tf_op jit(solution)/shard_map/ppermute | solution.py:243
  122.8 2.5 %collective-permute-start.22 = (bf16[64,7168]{1,0:T(8,128)(2,1)S(1)}, bf16[64,7168]{1,0:T(8,128)(2,1)S(1)}, u32[]{:S(2)}, u32[]{:S(2)}) collective-permute-start(bf16[64,7168]{1,0:T(8,128)(2,1)S(1)} %collective-permute-done.21.refs_6_), channel_id=1, source_target_pairs={{0,1},{1,0},{2,3},{3,2},{4,5},{5,4},{6,7},{7,6},{8,9},{9,8},{10,11... | collective-permute-start | bytes 2752520 | tf_op jit(solution)/shard_map/ppermute | solution.py:256
  124.0 2.6 %collective-permute-start.20 = (bf16[64,7168]{1,0:T(8,128)(2,1)S(1)}, bf16[64,7168]{1,0:T(8,128)(2,1)S(1)}, u32[]{:S(2)}, u32[]{:S(2)}) collective-permute-start(bf16[64,7168]{1,0:T(8,128)(2,1)S(1)} %collective-permute-done.15.refs_4_), channel_id=1, source_target_pairs={{0,1},{1,0},{2,3},{3,2},{4,5},{5,4},{6,7},{7,6},{8,9},{9,8},{10,11... | collective-permute-start | bytes 2752520 | tf_op jit(solution)/shard_map/ppermute | solution.py:256

commit v3 on v2

--- a/solution.py
+++ b/solution.py
@@ -48,7 +48,7 @@
 
 def input_kernel(n_row, n_col, slot_of, blocks, *refs):
     parts, refs = refs[:n_row], refs[n_row:]
-    sums, (send, dense, natural, grad) = refs[:n_col // 2], refs[n_col // 2:]
+    sums, (dense, natural, grad) = refs[:n_col], refs[n_col:]
     step = pl.program_id(0)
     tile, cols = dense.shape
     block = blocks.shape[1]
@@ -76,7 +76,6 @@
     part = lax.dot_general(grad[...], dense[...], (((1,), (1,)), ((), ())), preferred_element_type=jnp.float32)
     for place, ref in enumerate(sums):
         ref[...] = part[place * group:(place + 1) * group].astype(ref.dtype)
-    send[...] = part[n_col // 2 * group:].astype(send.dtype)
 
 
 def input_partial(n_row, n_col, slot_of, blocks, parts, rows):
@@ -84,9 +83,8 @@
     tokens = part_rows * n_row
     kind = blocks.dtype
     tile = tile_of(rows, blocks.shape[1], 1792)
-    group, n_hi = tokens // n_col, n_col // 2
-    shapes = [jax.ShapeDtypeStruct((height, rows), kind) for height in [group] * n_hi + [tokens // 2]]
-    specs = [pl.BlockSpec((height, tile), lambda t: (0, t)) for height in [group] * n_hi + [tokens // 2]]
+    shapes = [jax.ShapeDtypeStruct((tokens // n_col, rows), kind)] * n_col
+    specs = [pl.BlockSpec((tokens // n_col, tile), lambda t: (0, t))] * n_col
     return pl.pallas_call(
         functools.partial(input_kernel, n_row, n_col),
         grid=(rows // tile,),
@@ -95,9 +93,50 @@
         out_specs=(*specs, pl.BlockSpec((tile, cols), lambda t: (t, 0))),
         scratch_shapes=[pltpu.VMEM((tokens, cols), kind), pltpu.VMEM((tokens, cols), kind)],
         compiler_params=params(44),
-        cost_estimate=COST,
+        cost_estimate=pl.CostEstimate(flops=16 * tokens * rows * cols, bytes_accessed=8 * rows * cols, transcendentals=0),
         name="input_partial",
     )(slot_of, blocks, *parts)
+
+
+def pack_kernel(hidden, grad, out):
+    group, rows = hidden.shape
+    cols = grad.shape[1]
+    out[:, :rows] = hidden[...]
+    for strip in range(grad.shape[0] // group):
+        out[:, rows + strip * cols:rows + (strip + 1) * cols] = grad[strip * group:(strip + 1) * group, :]
+
+
+def pack(hidden, grad):
+    group, rows = hidden.shape
+    return pl.pallas_call(
+        pack_kernel,
+        out_shape=jax.ShapeDtypeStruct((group, rows + grad.size // group), hidden.dtype),
+        in_specs=[whole(pltpu.VMEM)] * 2,
+        out_specs=whole(pltpu.VMEM),
+        compiler_params=params(8),
+        cost_estimate=COST,
+        name="pack",
+    )(hidden, grad)
+
+
+def pair_kernel(one, two, out):
+    out[...] = (one[...].astype(jnp.float32) + two[...].astype(jnp.float32)).astype(out.dtype)
+
+
+def pair_sum(one, two):
+    height, rows = one.shape
+    tile = tile_of(rows, 128, 3584)
+    spec = pl.BlockSpec((height, tile), lambda t: (0, t))
+    return pl.pallas_call(
+        pair_kernel,
+        grid=(rows // tile,),
+        out_shape=jax.ShapeDtypeStruct(one.shape, one.dtype),
+        in_specs=[spec, spec],
+        out_specs=spec,
+        compiler_params=params(8),
+        cost_estimate=COST,
+        name="pair_sum",
+    )(one, two)
 
 
 def output_kernel(n_col, *refs):
@@ -135,7 +174,7 @@
         out_specs=pl.BlockSpec((tokens, cols), lambda t: (0, 0)),
         scratch_shapes=[pltpu.VMEM((tokens, cols), jnp.float32)],
         compiler_params=params(20),
-        cost_estimate=COST,
+        cost_estimate=pl.CostEstimate(flops=16 * tokens * rows * cols, bytes_accessed=8 * rows * cols, transcendentals=0),
         name="output_partial",
     )(*pieces, dense)
 
@@ -175,7 +214,7 @@
                 offset += group
             ref += choices * n_row
 
-    at_once = max(size for size in (1, 2, 4, 5, 8) if some_slots % size == 0)
+    at_once = max(size for size in (1, 2, 4, 5, 8, 10, 20) if some_slots % size == 0)
 
     def some(turn, carry):
         results = []
@@ -206,7 +245,7 @@
     held = [part for entry in work for parts in entry[0] for part in parts]
     pieces = [piece for entry in work for piece in entry[2]]
     tokens = pieces[0].shape[0] * len(pieces)
-    some_slots = share // 5 if share % 5 == 0 else share
+    some_slots = share // 4 if share % 4 == 0 else share
     spec = pl.BlockSpec((some_slots, block, block), lambda t: (t, 0, 0))
     extra = [] if first else [before]
     return pl.pallas_call(
@@ -277,28 +316,21 @@
     own_parts = all_rows(cotangent)
     if line:
         ends, middle, outward = [(0, 1), (1, 0), (2, 3), (3, 2)], [(1, 2), (2, 1)], [(1, 0), (2, 3)]
-        strips = range(0, part_rows, group)
-        packed = jnp.concatenate([hidden] + [cotangent[start:start + group] for start in strips], axis=1)
+        packed = pack(hidden, cotangent)
         hop_a, hop_b = along(packed, ends), along(packed, middle)
-    *sums, send, dense = input_partial(n_row, n_col, slot_of, blocks, own_parts, rows)
-
-    got = swap(send)
+    *sums, dense = input_partial(n_row, n_col, slot_of, blocks, own_parts, rows)
+
+    crossing = [pair_sum(sums[step], after(swap(sums[n_hi + step]), *near[1:])) for step in range(1, n_hi)]
     if line:
-        hop_a, hop_b = after(hop_a, send), after(hop_b, send)
+        hop_a, hop_b = after(hop_a, *crossing), after(hop_b, *crossing)
         hop_c, hop_d = along(hop_b, outward), along(hop_a, middle)
-        swapped = [swap(after(hidden, send, hop_a, hop_b, *near[1:]))]
+        swapped = [swap(after(hidden, hop_a, hop_b))]
     else:
         swapped = [swap(hidden)]
     for value in near[1:]:
-        swapped.append(swap(after(value, swapped[-1])))
+        swapped.append(swap(after(value, hop_a, hop_b) if line else value))
     own = near + swapped
-    got = after(got, *own)
-
-    def pair(step):
-        return sums[step].astype(jnp.float32) + got[step * group:(step + 1) * group].astype(jnp.float32)
-
-    crossing = [pair(step).astype(jnp.bfloat16) for step in range(1, n_hi)]
-    input_grad = pair(0)
+    input_grad = sums[0].astype(jnp.float32) + after(swap(after(sums[n_hi], *crossing)), *own).astype(jnp.float32)
     for step, value in enumerate(crossing):
         input_grad = input_grad + to_x(value, step + 1).astype(jnp.float32)
     input_grad = input_grad.astype(jnp.bfloat16)

time: 134 us -> 128 us (0.955)
  other arithmetic: 9.8 us -> 4.71 us
  waiting for transfers between devices: 51.1 us -> 55.7 us
  Pallas kernels: 41.5 us -> 38.5 us
  starting transfers between devices: 20.6 us -> 18.2 us
    ppermute x3, waiting for transfers between devices: 1.91 us -> 14.1 us  [from_x(): lax.ppermute(value, 'col', [((index // 2 + step) % n_hi * 2 + index % 2,...]
    ppermute x4, waiting for transfers between devices: 19.7 us -> 7.74 us  [shift(): lax.ppermute(value, axis, [(index, (index + step) % size) for index in ra...]
    ppermute x1, waiting for transfers between devices: 0.01 us -> 7.56 us  [to_x(): lax.ppermute(value, 'col', [(index, (index // 2 + step) % n_hi * 2 + inde...]
    pallas_call x3, Pallas kernels: 19.9 us -> 16.2 us  [weight_partial(): pl.pallas_call(functools.partial(weight_kernel, n_dp, n_row, n_col, plan,...]
    ppermute x6, waiting for transfers between devices: 22.2 us -> 19.6 us  [along(): return lax.ppermute(value, 'dp', pairs)]
    concatenate x1 -> x0, other arithmetic: 2.3 us -> none  [on_device(): jnp.concatenate([hidden] + [cotangent[start:start + group] for start in s...]
    unnamed x14 -> x20, local copies, waits for them, and re-layouts: 7.06 us -> 9.19 us
    ppermute x6, starting transfers between devices: 8.51 us -> 6.7 us  [along(): return lax.ppermute(value, 'dp', pairs)]
  transfers between devices with their start and end apart: 23 -> 24, of which waited for: 14 -> 12; matrix products, arithmetic and copies ran while one was open for 6% -> 4% of each run, Pallas kernels for 26% -> 26%
where the time goes in v3:
time: 128 us; the launch traced here: 127 us
  waiting for transfers between devices  55.7 us (44%)
  Pallas kernels  38.5 us (30%)
  starting transfers between devices  18.2 us (14%)
  local copies, waits for them, and re-layouts  9.31 us (7%)
  other arithmetic  4.71 us (4%)
    ppermute x6, waiting for transfers between devices, along(): return lax.ppermute(value, 'dp', pairs)  19.6 us
    pallas_call x3, Pallas kernels, weight_partial(): pl.pallas_call(functools.partial(weight_kernel, n_dp, n_row, n_col, plan,...  16.2 us
    pallas_call x1, Pallas kernels, input_partial(): pl.pallas_call(functools.partial(input_kernel, n_row, n_col), grid=(rows...  15.6 us
    ppermute x3, waiting for transfers between devices, from_x(): lax.ppermute(value, 'col', [((index // 2 + step) % n_hi * 2 + index % 2,...  14.1 us
    unnamed x20, local copies, waits for them, and re-layouts  9.19 us
    ppermute x4, waiting for transfers between devices, shift(): lax.ppermute(value, axis, [(index, (index + step) % size) for index in ra...  7.74 us
    ppermute x1, waiting for transfers between devices, to_x(): lax.ppermute(value, 'col', [(index, (index // 2 + step) % n_hi * 2 + inde...  7.56 us
    ppermute x6, starting transfers between devices, along(): return lax.ppermute(value, 'dp', pairs)  6.7 us
  transfers between devices with their start and end apart: 24, of which 12 were waited for; matrix products, arithmetic and copies ran while one was open for 4% of the time, Pallas kernels for 26%

profile of v3, /device:TPU:0, one launch (start us, length us, event | category | flops | bytes accessed | tf_op | source)
XLA Modules:
  0.0 127.3 jit_solution(14813313340357827081)
XLA Ops:
  0.6 3.0 %collective-permute-start.2 = (bf16[128,1024]{1,0:T(8,128)(2,1)}, bf16[128,1024]{1,0:T(8,128)(2,1)}, u32[]{:S(2)}, u32[]{:S(2)}) collective-permute-start(bf16[128,1024]{1,0:T(8,128)(2,1)} %refs_0_.4), channel_id=1, source_target_pairs={{0,4},{4,0},{1,5},{5,1},{2,6},{6,2},{3,7},{7,3},{8,12},{12,8},{9,1... | collective-permute-start | bytes 786440 | tf_op jit(solution)/shard_map/ppermute | solution.py:282
  3.7 1.5 %collective-permute-start = (bf16[64,7168]{1,0:T(8,128)(2,1)}, bf16[64,7168]{1,0:T(8,128)(2,1)}, u32[]{:S(2)}, u32[]{:S(2)}) collective-permute-start(bf16[64,7168]{1,0:T(8,128)(2,1)} %refs_2_.1), channel_id=1, source_target_pairs={{2,0},{3,1},{0,2},{1,3},{6,4},{7,5},{4,6},{5,7},{10,8},{11,9},{8,1... | collective-permute-start | bytes 2752520 | tf_op jit(solution)/shard_map/ppermute | solution.py:285
  5.2 1.2 copy-done
  6.4 0.9 copy-done.2
  7.3 0.1 pack.1
  7.4 1.6 %collective-permute-start.1 = (bf16[64,9216]{1,0:T(8,128)(2,1)S(1)}, bf16[64,9216]{1,0:T(8,128)(2,1)S(1)}, u32[]{:S(2)}, u32[]{:S(2)}) collective-permute-start(bf16[64,9216]{1,0:T(8,128)(2,1)S(1)} %pack.1), channel_id=1, source_target_pairs={{0,8},{8,0},{16,24},{24,16},{1,9},{9,1},{17,25},{25,17},{2,10},{10... | collective-permute-start | bytes 3538952 | tf_op jit(solution)/shard_map/ppermute | solution.py:304
  9.0 1.7 %collective-permute-start.4 = (bf16[64,9216]{1,0:T(8,128)(2,1)S(1)}, bf16[64,9216]{1,0:T(8,128)(2,1)}, u32[]{:S(2)}, u32[]{:S(2)}) collective-permute-start(bf16[64,9216]{1,0:T(8,128)(2,1)S(1)} %pack.1), channel_id=1, source_target_pairs={{8,16},{16,8},{9,17},{17,9},{10,18},{18,10},{11,19},{19,11},{12,20... | collective-permute-start | bytes 3538952 | tf_op jit(solution)/shard_map/ppermute | solution.py:304
  10.8 0.2 select_reduce_fusion.slot_of
  10.9 0.0 collective-permute-done.2.refs_1_
  11.0 15.6 %input_partial.1 = (bf16[64,7168]{1,0:T(8,128)(2,1)S(1)}, bf16[64,7168]{1,0:T(8,128)(2,1)S(1)}, bf16[64,7168]{1,0:T(8,128)(2,1)S(1)}, bf16[64,7168]{1,0:T(8,128)(2,1)S(1)}, bf16[7168,1024]{1,0:T(8,128)(2,1)}) custom-call(s32[448]{0:T(512)S(1)} %select_reduce_fusion.slot_of, bf16[320,128,128]{2,1,0:T(8,128)(2,1)} %bitcast.11, ...), custom_call_target="tpu_custom_call" | custom-call | flops 30064771072 | bytes 58720256 | tf_op jit(solution)/shard_map/input_partial/pallas_call | solution.py:88
  26.5 0.9 copy-done.7
  27.4 0.0 collective-permute-start.3
  27.4 0.0 collective-permute-done.refs_1_.refs_3_
  27.4 2.5 %collective-permute-done.3.two = bf16[64,7168]{1,0:T(8,128)(2,1)S(1)} collective-permute-done((bf16[64,7168]{1,0:T(8,128)(2,1)S(1)}, bf16[64,7168]{1,0:T(8,128)(2,1)S(1)}, u32[]{:S(2)}, u32[]{:S(2)}) %collective-permute-start.3) | collective-permute-done | bytes 917536 | tf_op jit(solution)/shard_map/ppermute | solution.py:295
  29.9 0.4 pair_sum.1
  30.4 0.0 copy-start.6
  30.4 0.9 copy-done.6
  31.3 3.3 %collective-permute-done.1.refs_6_ = bf16[64,9216]{1,0:T(8,128)(2,1)S(1)} collective-permute-done((bf16[64,9216]{1,0:T(8,128)(2,1)S(1)}, bf16[64,9216]{1,0:T(8,128)(2,1)S(1)}, u32[]{:S(2)}, u32[]{:S(2)}) %collective-permute-start.1) | collective-permute-done | bytes 1179680 | tf_op jit(solution)/shard_map/ppermute | solution.py:304
  34.6 0.0 collective-permute-done.4
  34.6 0.0 collective-permute-start.5
  34.6 0.5 collective-permute-start.6
  35.1 0.5 collective-permute-start.8
  35.7 1.3 %collective-permute-start.10 = (bf16[64,9216]{1,0:T(8,128)(2,1)}, bf16[64,9216]{1,0:T(8,128)(2,1)S(1)}, u32[]{:S(2)}, u32[]{:S(2)}) collective-permute-start(bf16[64,9216]{1,0:T(8,128)(2,1)} %collective-permute-done.4), channel_id=1, source_target_pairs={{8,0},{16,24},{9,1},{17,25},{10,2},{18,26},{11,3},{19,27},{12,4},{... | collective-permute-start | bytes 3538952 | tf_op jit(solution)/shard_map/ppermute | solution.py:304
  37.0 0.7 collective-permute-start.12
  37.7 0.0 collective-permute-done.5.refs_2_.refs_4_
  37.7 0.1 collective-permute-start.7
  37.8 0.9 collective-permute-done.6.refs_3_.refs_5_
  38.8 5.2 %copy-done.8 = bf16[7168,1024]{1,0:T(8,128)(2,1)S(1)} copy-done((bf16[7168,1024]{1,0:T(8,128)(2,1)S(1)}, bf16[7168,1024]{1,0:T(8,128)(2,1)}, u32[]{:S(2)}) %copy-start.8) | copy-done | bytes 14680088
  43.9 6.2 %output_partial.1 = bf16[256,1024]{1,0:T(8,128)(2,1)S(1)} custom-call(bf16[64,7168]{1,0:T(8,128)(2,1)S(1)} %copy-done.1, bf16[64,7168]{1,0:T(8,128)(2,1)} %collective-permute-done.refs_1_.refs_3_, bf16[64,7168]{1,0:T(8,128)(2,1)S(1)} %collective-permute-done.5.refs_2_.refs_4_, bf16[64,7168]{1,0:T(8,128)(2,1)} %collective-permute-done.6.refs_3_.refs_5_, ...), custom_call_target="tpu_custom_call" | custom-call | flops 30064771072 | bytes 58720256 | tf_op jit(solution)/shard_map/output_partial/pallas_call | solution.py:169
  50.1 0.0 collective-permute-done.7
  50.1 7.6 %collective-permute-done.8 = bf16[64,7168]{1,0:T(8,128)(2,1)S(1)} collective-permute-done((bf16[64,7168]{1,0:T(8,128)(2,1)}, bf16[64,7168]{1,0:T(8,128)(2,1)S(1)}, u32[]{:S(2)}, u32[]{:S(2)}) %collective-permute-start.8) | collective-permute-done | bytes 917536 | tf_op jit(solution)/shard_map/ppermute | solution.py:290
  57.7 1.3 add_convert_fusion
  59.0 0.6 collective-permute-start.9
  59.5 8.2 %collective-permute-done.10 = bf16[64,9216]{1,0:T(8,128)(2,1)S(1)} collective-permute-done((bf16[64,9216]{1,0:T(8,128)(2,1)}, bf16[64,9216]{1,0:T(8,128)(2,1)S(1)}, u32[]{:S(2)}, u32[]{:S(2)}) %collective-permute-start.10) | collective-permute-done | bytes 1179680 | tf_op jit(solution)/shard_map/ppermute | solution.py:304
  67.7 0.0 collective-permute-done.12
  67.7 1.3 %collective-permute-start.13 = (bf16[64,9216]{1,0:T(8,128)(2,1)S(1)}, bf16[64,9216]{1,0:T(8,128)(2,1)S(1)}, u32[]{:S(2)}, u32[]{:S(2)}) collective-permute-start(bf16[64,9216]{1,0:T(8,128)(2,1)S(1)} %collective-permute-done.12), channel_id=1, source_target_pairs={{8,0},{16,24},{9,1},{17,25},{10,2},{18,26},{11,3},{19,27},{12,4},{... | collective-permute-start | bytes 3538952 | tf_op jit(solution)/shard_map/ppermute | solution.py:304
  69.0 1.3 %slice_select_fusion.1.refs_8_ = bf16[64,7168]{1,0:T(8,128)(2,1)S(1)} fusion(bf16[64,9216]{1,0:T(8,128)(2,1)S(1)} %collective-permute-done.10, bf16[64,9216]{1,0:T(8,128)(2,1)} %collective-permute-done.4, pred[]{:T(512)S(6)} %or.3), kind=kLoop, calls=%fused_computation.2 | loop fusion | flops 458752 | bytes 2752513 | tf_op jit(solution)/shard_map/jit(_where)/select_n | solution.py:352
  70.3 1.0 slice_select_fusion.3
  71.3 1.6 %collective-permute-start.14 = (bf16[64,7168]{1,0:T(8,128)(2,1)S(1)}, bf16[64,7168]{1,0:T(8,128)(2,1)S(1)}, u32[]{:S(2)}, u32[]{:S(2)}) collective-permute-start(bf16[64,7168]{1,0:T(8,128)(2,1)S(1)} %slice_select_fusion.1.refs_8_), channel_id=1, source_target_pairs={{2,0},{3,1},{0,2},{1,3},{6,4},{7,5},{4,6},{5,7},{10,8},{11,9},{8,1... | collective-permute-start | bytes 2752520 | tf_op jit(solution)/shard_map/ppermute | solution.py:285
  72.9 0.6 collective-permute-start.11
  73.5 0.0 collective-permute-done.9
  73.5 0.8 fusion
  74.3 4.8 %weight_partial.3.refs_14_ = f32[80,128,128]{2,1,0:T(8,128)S(1)} custom-call(s32[320]{0:T(512)S(1)} %reduce.kept, bf16[128,1024]{1,0:T(8,128)(2,1)S(1)} %copy-done.3, bf16[128,1024]{1,0:T(8,128)(2,1)} %collective-permute-done.2.refs_1_, bf16[64,7168]{1,0:T(8,128)(2,1)S(1)} %copy-done.1, bf16[64,7168]{1,0:T(8,128)(2,1)} %collective-permute-done.refs_1_.refs_3_, ...), custom_call_target="tpu_custom_call" | custom-call | flops 1000 | bytes 1000 | tf_op jit(solution)/shard_map/weight_partial/pallas_call | solution.py:251
  79.1 13.7 %collective-permute-done.14.refs_9_ = bf16[64,7168]{1,0:T(8,128)(2,1)S(1)} collective-permute-done((bf16[64,7168]{1,0:T(8,128)(2,1)S(1)}, bf16[64,7168]{1,0:T(8,128)(2,1)S(1)}, u32[]{:S(2)}, u32[]{:S(2)}) %collective-permute-start.14) | collective-permute-done | bytes 917536 | tf_op jit(solution)/shard_map/ppermute | solution.py:285
  92.8 0.0 collective-permute-start.17
  92.8 0.5 collective-permute-start.18
  93.3 4.2 %collective-permute-done.13 = bf16[64,9216]{1,0:T(8,128)(2,1)S(1)} collective-permute-done((bf16[64,9216]{1,0:T(8,128)(2,1)S(1)}, bf16[64,9216]{1,0:T(8,128)(2,1)S(1)}, u32[]{:S(2)}, u32[]{:S(2)}) %collective-permute-start.13) | collective-permute-done | bytes 1179680 | tf_op jit(solution)/shard_map/ppermute | solution.py:304
  97.5 0.1 slice_select_fusion.refs_12_
  97.6 0.1 collective-permute-start.16
  97.7 1.6 %collective-permute-start.22 = (bf16[64,7168]{1,0:T(8,128)(2,1)S(1)}, bf16[64,7168]{1,0:T(8,128)(2,1)S(1)}, u32[]{:S(2)}, u32[]{:S(2)}) collective-permute-start(bf16[64,7168]{1,0:T(8,128)(2,1)S(1)} %slice_select_fusion.refs_12_), channel_id=1, source_target_pairs={{2,0},{3,1},{0,2},{1,3},{6,4},{7,5},{4,6},{5,7},{10,8},{11,9},{8,1... | collective-permute-start | bytes 2752520 | tf_op jit(solution)/shard_map/ppermute | solution.py:285
  99.2 0.0 collective-permute-start.19
  99.2 0.5 collective-permute-start.20
  99.8 0.0 collective-permute-done.11
  99.8 0.6 collective-permute-start.15
  100.4 7.7 %collective-permute-done.15.refs_5_.refs_3_ = bf16[64,2048]{1,0:T(8,128)(2,1)S(1)} collective-permute-done((bf16[64,2048]{1,0:T(8,128)(2,1)S(1)}, bf16[64,2048]{1,0:T(8,128)(2,1)S(1)}, u32[]{:S(2)}, u32[]{:S(2)}) %collective-permute-start.15) | collective-permute-done | bytes 262176 | tf_op jit(solution)/shard_map/ppermute | solution.py:282
  108.1 0.0 collective-permute-done.19.refs_11_
  108.1 6.3 %weight_partial.4.refs_8_ = f32[80,128,128]{2,1,0:T(8,128)S(1)} custom-call(s32[320]{0:T(512)S(1)} %reduce.kept, bf16[64,2048]{1,0:T(8,128)(2,1)S(1)} %get-tuple-element.64.refs_0_, bf16[64,2048]{1,0:T(8,128)(2,1)S(1)} %get-tuple-element.62.refs_1_, bf16[64,2048]{1,0:T(8,128)(2,1)S(1)} %get-tuple-element.63.refs_2_, ...), custom_call_target="tpu_custom_call" | custom-call | flops 1000 | bytes 1000 | tf_op jit(solution)/shard_map/weight_partial/pallas_call | solution.py:251
  114.4 3.9 %collective-permute-done.16.refs_4_ = bf16[64,7168]{1,0:T(8,128)(2,1)S(1)} collective-permute-done((bf16[64,7168]{1,0:T(8,128)(2,1)}, bf16[64,7168]{1,0:T(8,128)(2,1)S(1)}, u32[]{:S(2)}, u32[]{:S(2)}) %collective-permute-start.16) | collective-permute-done | bytes 917536 | tf_op jit(solution)/shard_map/ppermute | solution.py:304
  118.3 0.0 collective-permute-start.21
  118.3 0.4 collective-permute-done.22.refs_6_
  118.7 0.1 collective-permute-start.23
  118.8 2.0 %collective-permute-done.21.refs_5_ = bf16[64,7168]{1,0:T(8,128)(2,1)S(1)} collective-permute-done((bf16[64,7168]{1,0:T(8,128)(2,1)S(1)}, bf16[64,7168]{1,0:T(8,128)(2,1)S(1)}, u32[]{:S(2)}, u32[]{:S(2)}) %collective-permute-start.21) | collective-permute-done | bytes 917536 | tf_op jit(solution)/shard_map/ppermute | solution.py:295
  120.8 1.3 %collective-permute-done.23.refs_7_ = bf16[64,7168]{1,0:T(8,128)(2,1)S(1)} collective-permute-done((bf16[64,7168]{1,0:T(8,128)(2,1)S(1)}, bf16[64,7168]{1,0:T(8,128)(2,1)S(1)}, u32[]{:S(2)}, u32[]{:S(2)}) %collective-permute-start.23) | collective-permute-done | bytes 917536 | tf_op jit(solution)/shard_map/ppermute | solution.py:295
  122.1 5.2 %weight_partial.5 = bf16[80,128,128]{2,1,0:T(8,128)(2,1)} custom-call(s32[320]{0:T(512)S(1)} %reduce.kept, bf16[64,2048]{1,0:T(8,128)(2,1)S(1)} %get-tuple-element.64.refs_0_, bf16[64,2048]{1,0:T(8,128)(2,1)S(1)} %get-tuple-element.62.refs_1_, bf16[64,2048]{1,0:T(8,128)(2,1)S(1)} %slice_select_fusion.2.refs_4_.refs_2_, ...), custom_call_target="tpu_custom_call" | custom-call | flops 1000 | bytes 1000 | tf_op jit(solution)/shard_map/weight_partial/pallas_call | solution.py:251
  (24 shorter events, 0.2 us)
Async XLA Ops:
  0.6 10.3 %collective-permute-start.2 = (bf16[128,1024]{1,0:T(8,128)(2,1)}, bf16[128,1024]{1,0:T(8,128)(2,1)}, u32[]{:S(2)}, u32[]{:S(2)}) collective-permute-start(bf16[128,1024]{1,0:T(8,128)(2,1)} %refs_0_.4), channel_id=1, source_target_pairs={{0,4},{4,0},{1,5},{5,1},{2,6},{6,2},{3,7},{7,3},{8,12},{12,8},{9,1... | collective-permute-start | bytes 786440 | tf_op jit(solution)/shard_map/ppermute | solution.py:282
  3.7 23.8 %collective-permute-start = (bf16[64,7168]{1,0:T(8,128)(2,1)}, bf16[64,7168]{1,0:T(8,128)(2,1)}, u32[]{:S(2)}, u32[]{:S(2)}) collective-permute-start(bf16[64,7168]{1,0:T(8,128)(2,1)} %refs_2_.1), channel_id=1, source_target_pairs={{2,0},{3,1},{0,2},{1,3},{6,4},{7,5},{4,6},{5,7},{10,8},{11,9},{8,1... | collective-permute-start | bytes 2752520 | tf_op jit(solution)/shard_map/ppermute | solution.py:285
  5.2 1.2 copy-start
  6.4 0.9 copy-start.2
  7.3 3.4 %copy-start.9 = (s32[1,1,320]{2,1,0:T(1,128)S(1)}, s32[1,1,320]{2,1,0:T(1,128)}, u32[]{:S(2)}) copy-start(s32[1,1,320]{2,1,0:T(1,128)} %param.6) | copy-start | bytes 3844
  7.3 3.6 %copy-start.3 = (bf16[128,1024]{1,0:T(8,128)(2,1)S(1)}, bf16[128,1024]{1,0:T(8,128)(2,1)}, u32[]{:S(2)}) copy-start(bf16[128,1024]{1,0:T(8,128)(2,1)} %refs_0_.4) | copy-start | bytes 786436
  7.4 27.2 %collective-permute-start.1 = (bf16[64,9216]{1,0:T(8,128)(2,1)S(1)}, bf16[64,9216]{1,0:T(8,128)(2,1)S(1)}, u32[]{:S(2)}, u32[]{:S(2)}) collective-permute-start(bf16[64,9216]{1,0:T(8,128)(2,1)S(1)} %pack.1), channel_id=1, source_target_pairs={{0,8},{8,0},{16,24},{24,16},{1,9},{9,1},{17,25},{25,17},{2,10},{10... | collective-permute-start | bytes 3538952 | tf_op jit(solution)/shard_map/ppermute | solution.py:304
  9.0 25.6 %collective-permute-start.4 = (bf16[64,9216]{1,0:T(8,128)(2,1)S(1)}, bf16[64,9216]{1,0:T(8,128)(2,1)}, u32[]{:S(2)}, u32[]{:S(2)}) collective-permute-start(bf16[64,9216]{1,0:T(8,128)(2,1)S(1)} %pack.1), channel_id=1, source_target_pairs={{8,16},{16,8},{9,17},{17,9},{10,18},{18,10},{11,19},{19,11},{12,20... | collective-permute-start | bytes 3538952 | tf_op jit(solution)/shard_map/ppermute | solution.py:304
  26.5 0.9 copy-start.7
  27.4 2.9 %copy-start.4 = (bf16[64,7168]{1,0:T(8,128)(2,1)}, bf16[64,7168]{1,0:T(8,128)(2,1)S(1)}, u32[]{:S(2)}) copy-start(bf16[64,7168]{1,0:T(8,128)(2,1)S(1)} %get-tuple-element.41) | copy-start | bytes 2752516
  27.4 2.5 %collective-permute-start.3 = (bf16[64,7168]{1,0:T(8,128)(2,1)S(1)}, bf16[64,7168]{1,0:T(8,128)(2,1)S(1)}, u32[]{:S(2)}, u32[]{:S(2)}) collective-permute-start(bf16[64,7168]{1,0:T(8,128)(2,1)S(1)} %get-tuple-element.33), channel_id=1, source_target_pairs={{0,1},{1,0},{2,3},{3,2},{4,5},{5,4},{6,7},{7,6},{8,9},{9,8},{10,11... | collective-permute-start | bytes 2752520 | tf_op jit(solution)/shard_map/ppermute | solution.py:295
  29.9 4.7 %copy-start.1 = (bf16[64,7168]{1,0:T(8,128)(2,1)S(1)}, bf16[64,7168]{1,0:T(8,128)(2,1)}, u32[]{:S(2)}) copy-start(bf16[64,7168]{1,0:T(8,128)(2,1)} %refs_2_.1) | copy-start | bytes 2752516
  30.4 0.9 copy-start.6
  34.6 3.1 %collective-permute-start.5 = (bf16[64,7168]{1,0:T(8,128)(2,1)S(1)}, bf16[64,7168]{1,0:T(8,128)(2,1)S(1)}, u32[]{:S(2)}, u32[]{:S(2)}) collective-permute-start(bf16[64,7168]{1,0:T(8,128)(2,1)S(1)} %copy-done.1), channel_id=1, source_target_pairs={{0,1},{1,0},{2,3},{3,2},{4,5},{5,4},{6,7},{7,6},{8,9},{9,8},{10,11... | collective-permute-start | bytes 2752520 | tf_op jit(solution)/shard_map/ppermute | solution.py:295
  34.6 4.1 %collective-permute-start.6 = (bf16[64,7168]{1,0:T(8,128)(2,1)}, bf16[64,7168]{1,0:T(8,128)(2,1)}, u32[]{:S(2)}, u32[]{:S(2)}) collective-permute-start(bf16[64,7168]{1,0:T(8,128)(2,1)} %collective-permute-done.refs_1_.refs_3_), channel_id=1, source_target_pairs={{0,1},{1,0},{2,3},{3,2},{4,5},{5,4},{6,7},{7,6},{8,9},{9,8},{10,11... | collective-permute-start | bytes 2752520 | tf_op jit(solution)/shard_map/ppermute | solution.py:295
  35.1 22.5 %collective-permute-start.8 = (bf16[64,7168]{1,0:T(8,128)(2,1)}, bf16[64,7168]{1,0:T(8,128)(2,1)S(1)}, u32[]{:S(2)}, u32[]{:S(2)}) collective-permute-start(bf16[64,7168]{1,0:T(8,128)(2,1)} %copy-done.6), channel_id=1, source_target_pairs={{0,2},{1,3},{2,0},{3,1},{4,6},{5,7},{6,4},{7,5},{8,10},{9,11},{10,... | collective-permute-start | bytes 2752520 | tf_op jit(solution)/shard_map/ppermute | solution.py:290
  35.7 32.0 %collective-permute-start.10 = (bf16[64,9216]{1,0:T(8,128)(2,1)}, bf16[64,9216]{1,0:T(8,128)(2,1)S(1)}, u32[]{:S(2)}, u32[]{:S(2)}) collective-permute-start(bf16[64,9216]{1,0:T(8,128)(2,1)} %collective-permute-done.4), channel_id=1, source_target_pairs={{8,0},{16,24},{9,1},{17,25},{10,2},{18,26},{11,3},{19,27},{12,4},{... | collective-permute-start | bytes 3538952 | tf_op jit(solution)/shard_map/ppermute | solution.py:304
  37.0 30.7 %collective-permute-start.12 = (bf16[64,9216]{1,0:T(8,128)(2,1)S(1)}, bf16[64,9216]{1,0:T(8,128)(2,1)S(1)}, u32[]{:S(2)}, u32[]{:S(2)}) collective-permute-start(bf16[64,9216]{1,0:T(8,128)(2,1)S(1)} %collective-permute-done.1.refs_6_), channel_id=1, source_target_pairs={{8,16},{16,8},{9,17},{17,9},{10,18},{18,10},{11,19},{19,11},{12,20... | collective-permute-start | bytes 3538952 | tf_op jit(solution)/shard_map/ppermute | solution.py:304
  37.7 19.9 %copy-start.5 = (bf16[64,7168]{1,0:T(8,128)(2,1)S(1)}, bf16[64,7168]{1,0:T(8,128)(2,1)}, u32[]{:S(2)}) copy-start(bf16[64,7168]{1,0:T(8,128)(2,1)} %copy-done.4) | copy-start | bytes 2752516
  37.7 12.4 %collective-permute-start.7 = (bf16[64,7168]{1,0:T(8,128)(2,1)}, bf16[64,7168]{1,0:T(8,128)(2,1)S(1)}, u32[]{:S(2)}, u32[]{:S(2)}) collective-permute-start(bf16[64,7168]{1,0:T(8,128)(2,1)} %copy-done.7), channel_id=1, source_target_pairs={{0,1},{1,0},{2,3},{3,2},{4,5},{5,4},{6,7},{7,6},{8,9},{9,8},{10,11... | collective-permute-start | bytes 2752520 | tf_op jit(solution)/shard_map/ppermute | solution.py:295
  38.8 5.2 %copy-start.8 = (bf16[7168,1024]{1,0:T(8,128)(2,1)S(1)}, bf16[7168,1024]{1,0:T(8,128)(2,1)}, u32[]{:S(2)}) copy-start(bf16[7168,1024]{1,0:T(8,128)(2,1)} %get-tuple-element.40.refs_4_) | copy-start | bytes 44040196
  59.0 14.5 %collective-permute-start.9 = (bf16[128,1024]{1,0:T(8,128)(2,1)S(1)}, bf16[128,1024]{1,0:T(8,128)(2,1)S(1)}, u32[]{:S(2)}, u32[]{:S(2)}) collective-permute-start(bf16[128,1024]{1,0:T(8,128)(2,1)S(1)} %dynamic-slice_bitcast_fusion), channel_id=1, source_target_pairs={{0,4},{4,0},{1,5},{5,1},{2,6},{6,2},{3,7},{7,3},{8,12},{12,8},{9,1... | collective-permute-start | bytes 786440 | tf_op jit(solution)/shard_map/ppermute | solution.py:282
  67.7 29.8 %collective-permute-start.13 = (bf16[64,9216]{1,0:T(8,128)(2,1)S(1)}, bf16[64,9216]{1,0:T(8,128)(2,1)S(1)}, u32[]{:S(2)}, u32[]{:S(2)}) collective-permute-start(bf16[64,9216]{1,0:T(8,128)(2,1)S(1)} %collective-permute-done.12), channel_id=1, source_target_pairs={{8,0},{16,24},{9,1},{17,25},{10,2},{18,26},{11,3},{19,27},{12,4},{... | collective-permute-start | bytes 3538952 | tf_op jit(solution)/shard_map/ppermute | solution.py:304
  71.3 21.5 %collective-permute-start.14 = (bf16[64,7168]{1,0:T(8,128)(2,1)S(1)}, bf16[64,7168]{1,0:T(8,128)(2,1)S(1)}, u32[]{:S(2)}, u32[]{:S(2)}) collective-permute-start(bf16[64,7168]{1,0:T(8,128)(2,1)S(1)} %slice_select_fusion.1.refs_8_), channel_id=1, source_target_pairs={{2,0},{3,1},{0,2},{1,3},{6,4},{7,5},{4,6},{5,7},{10,8},{11,9},{8,1... | collective-permute-start | bytes 2752520 | tf_op jit(solution)/shard_map/ppermute | solution.py:285
  72.9 26.8 %collective-permute-start.11 = (bf16[128,2048]{1,0:T(8,128)(2,1)S(1)}, bf16[128,2048]{1,0:T(8,128)(2,1)S(1)}, u32[]{:S(2)}, u32[]{:S(2)}) collective-permute-start(bf16[128,2048]{1,0:T(8,128)(2,1)S(1)} %pad_maximum_fusion), channel_id=1, source_target_pairs={{0,4},{4,0},{1,5},{5,1},{2,6},{6,2},{3,7},{7,3},{8,12},{12,8},{9,1... | collective-permute-start | bytes 1572872 | tf_op jit(solution)/shard_map/ppermute | solution.py:282
  92.8 6.4 %collective-permute-start.17 = (bf16[64,9216]{1,0:T(8,128)(2,1)S(1)}, bf16[64,9216]{1,0:T(8,128)(2,1)S(1)}, u32[]{:S(2)}, u32[]{:S(2)}) collective-permute-start(bf16[64,9216]{1,0:T(8,128)(2,1)S(1)} %collective-permute-done.1.refs_6_), channel_id=1, source_target_pairs={{0,1},{1,0},{2,3},{3,2},{4,5},{5,4},{6,7},{7,6},{8,9},{9,8},{10,11... | collective-permute-start | bytes 3538952 | tf_op jit(solution)/shard_map/ppermute | solution.py:295
  92.8 6.4 %collective-permute-start.18 = (bf16[64,7168]{1,0:T(8,128)(2,1)S(1)}, bf16[64,7168]{1,0:T(8,128)(2,1)S(1)}, u32[]{:S(2)}, u32[]{:S(2)}) collective-permute-start(bf16[64,7168]{1,0:T(8,128)(2,1)S(1)} %slice_select_fusion.1.refs_8_), channel_id=1, source_target_pairs={{0,1},{1,0},{2,3},{3,2},{4,5},{5,4},{6,7},{7,6},{8,9},{9,8},{10,11... | collective-permute-start | bytes 2752520 | tf_op jit(solution)/shard_map/ppermute | solution.py:295
  97.6 20.7 %collective-permute-start.16 = (bf16[64,7168]{1,0:T(8,128)(2,1)}, bf16[64,7168]{1,0:T(8,128)(2,1)S(1)}, u32[]{:S(2)}, u32[]{:S(2)}) collective-permute-start(bf16[64,7168]{1,0:T(8,128)(2,1)} %collective-permute-done.refs_1_.refs_3_), channel_id=1, source_target_pairs={{0,8},{8,0},{16,24},{24,16},{1,9},{9,1},{17,25},{25,17},{2,10},{10... | collective-permute-start | bytes 2752520 | tf_op jit(solution)/shard_map/ppermute | solution.py:304
  97.7 21.1 %collective-permute-start.22 = (bf16[64,7168]{1,0:T(8,128)(2,1)S(1)}, bf16[64,7168]{1,0:T(8,128)(2,1)S(1)}, u32[]{:S(2)}, u32[]{:S(2)}) collective-permute-start(bf16[64,7168]{1,0:T(8,128)(2,1)S(1)} %slice_select_fusion.refs_12_), channel_id=1, source_target_pairs={{2,0},{3,1},{0,2},{1,3},{6,4},{7,5},{4,6},{5,7},{10,8},{11,9},{8,1... | collective-permute-start | bytes 2752520 | tf_op jit(solution)/shard_map/ppermute | solution.py:285
  99.2 8.9 %collective-permute-start.19 = (bf16[64,7168]{1,0:T(8,128)(2,1)S(1)}, bf16[64,7168]{1,0:T(8,128)(2,1)S(1)}, u32[]{:S(2)}, u32[]{:S(2)}) collective-permute-start(bf16[64,7168]{1,0:T(8,128)(2,1)S(1)} %collective-permute-done.14.refs_9_), channel_id=1, source_target_pairs={{0,1},{1,0},{2,3},{3,2},{4,5},{5,4},{6,7},{7,6},{8,9},{9,8},{10,11... | collective-permute-start | bytes 2752520 | tf_op jit(solution)/shard_map/ppermute | solution.py:295
  99.2 8.9 %collective-permute-start.20 = (bf16[64,7168]{1,0:T(8,128)(2,1)S(1)}, bf16[64,7168]{1,0:T(8,128)(2,1)S(1)}, u32[]{:S(2)}, u32[]{:S(2)}) collective-permute-start(bf16[64,7168]{1,0:T(8,128)(2,1)S(1)} %slice_select_fusion.refs_12_), channel_id=1, source_target_pairs={{0,1},{1,0},{2,3},{3,2},{4,5},{5,4},{6,7},{7,6},{8,9},{9,8},{10,11... | collective-permute-start | bytes 2752520 | tf_op jit(solution)/shard_map/ppermute | solution.py:295
  99.8 8.3 %collective-permute-start.15 = (bf16[64,2048]{1,0:T(8,128)(2,1)S(1)}, bf16[64,2048]{1,0:T(8,128)(2,1)S(1)}, u32[]{:S(2)}, u32[]{:S(2)}) collective-permute-start(bf16[64,2048]{1,0:T(8,128)(2,1)S(1)} %slice_select_fusion.2.refs_4_.refs_2_), channel_id=1, source_target_pairs={{0,4},{4,0},{1,5},{5,1},{2,6},{6,2},{3,7},{7,3},{8,12},{12,8},{9,1... | collective-permute-start | bytes 786440 | tf_op jit(solution)/shard_map/ppermute | solution.py:282
  118.3 2.5 %collective-permute-start.21 = (bf16[64,7168]{1,0:T(8,128)(2,1)S(1)}, bf16[64,7168]{1,0:T(8,128)(2,1)S(1)}, u32[]{:S(2)}, u32[]{:S(2)}) collective-permute-start(bf16[64,7168]{1,0:T(8,128)(2,1)S(1)} %collective-permute-done.16.refs_4_), channel_id=1, source_target_pairs={{0,1},{1,0},{2,3},{3,2},{4,5},{5,4},{6,7},{7,6},{8,9},{9,8},{10,11... | collective-permute-start | bytes 2752520 | tf_op jit(solution)/shard_map/ppermute | solution.py:295
  118.7 3.3 %collective-permute-start.23 = (bf16[64,7168]{1,0:T(8,128)(2,1)S(1)}, bf16[64,7168]{1,0:T(8,128)(2,1)S(1)}, u32[]{:S(2)}, u32[]{:S(2)}) collective-permute-start(bf16[64,7168]{1,0:T(8,128)(2,1)S(1)} %collective-permute-done.22.refs_6_), channel_id=1, source_target_pairs={{0,1},{1,0},{2,3},{3,2},{4,5},{5,4},{6,7},{7,6},{8,9},{9,8},{10,11... | collective-permute-start | bytes 2752520 | tf_op jit(solution)/shard_map/ppermute | solution.py:295

commit v4 on v3

--- a/solution.py
+++ b/solution.py
@@ -312,11 +312,11 @@
         axis=1,
     )
     line = n_dp == 4 and n_hi == 2 and part_rows % group == 0
-    near = [hidden] + over_x(hidden)
+    packed = pack(hidden, cotangent) if line else hidden
+    near = [hidden] + over_x(after(hidden, packed))
     own_parts = all_rows(cotangent)
     if line:
         ends, middle, outward = [(0, 1), (1, 0), (2, 3), (3, 2)], [(1, 2), (2, 1)], [(1, 0), (2, 3)]
-        packed = pack(hidden, cotangent)
         hop_a, hop_b = along(packed, ends), along(packed, middle)
     *sums, dense = input_partial(n_row, n_col, slot_of, blocks, own_parts, rows)
 

time: 128 us -> 127 us (level)
    ppermute x3, waiting for transfers between devices: 14.1 us -> 18.8 us  [from_x(): lax.ppermute(value, 'col', [((index // 2 + step) % n_hi * 2 + index % 2,...]
    ppermute x10, waiting for transfers between devices: 6.67 us -> 3.14 us  [swap(): lax.ppermute(value, 'col', [(index, index ^ 1) for index in range(n_col)])]
    ppermute x3, starting transfers between devices: 4.6 us -> 2.69 us  [from_x(): lax.ppermute(value, 'col', [((index // 2 + step) % n_hi * 2 + index % 2,...]
    unnamed x20 -> x16, local copies, waits for them, and re-layouts: 9.19 us -> 8.06 us
  transfers between devices with their start and end apart: 24 -> 24, of which waited for: 12 -> 11; matrix products, arithmetic and copies ran while one was open for 4% -> 4% of each run, Pallas kernels for 26% -> 27%
where the time goes in v4:
time: 127 us
  waiting for transfers between devices  56.3 us (44%)
  Pallas kernels  39.7 us (31%)
  starting transfers between devices  17.1 us (13%)
  local copies, waits for them, and re-layouts  8.18 us (6%)
  other arithmetic  4.71 us (4%)
    ppermute x6, waiting for transfers between devices, along(): return lax.ppermute(value, 'dp', pairs)  19.2 us
    ppermute x3, waiting for transfers between devices, from_x(): lax.ppermute(value, 'col', [((index // 2 + step) % n_hi * 2 + index % 2,...  18.8 us
    pallas_call x3, Pallas kernels, weight_partial(): pl.pallas_call(functools.partial(weight_kernel, n_dp, n_row, n_col, plan,...  16.2 us
    pallas_call x1, Pallas kernels, input_partial(): pl.pallas_call(functools.partial(input_kernel, n_row, n_col), grid=(rows...  15.6 us
    unnamed x16, local copies, waits for them, and re-layouts  8.06 us
    ppermute x4, waiting for transfers between devices, shift(): lax.ppermute(value, axis, [(index, (index + step) % size) for index in ra...  7.74 us
    ppermute x1, waiting for transfers between devices, to_x(): lax.ppermute(value, 'col', [(index, (index // 2 + step) % n_hi * 2 + inde...  7.4 us
    ppermute x6, starting transfers between devices, along(): return lax.ppermute(value, 'dp', pairs)  6.71 us
  transfers between devices with their start and end apart: 24, of which 11 were waited for; matrix products, arithmetic and copies ran while one was open for 4% of the time, Pallas kernels for 27%

profile of v4, /device:TPU:0, one launch (start us, length us, event | category | flops | bytes accessed | tf_op | source)
XLA Modules:
  0.0 126.8 jit_solution(13996432831705837919)
XLA Ops:
  0.6 3.0 %collective-permute-start.2 = (bf16[128,1024]{1,0:T(8,128)(2,1)}, bf16[128,1024]{1,0:T(8,128)(2,1)}, u32[]{:S(2)}, u32[]{:S(2)}) collective-permute-start(bf16[128,1024]{1,0:T(8,128)(2,1)} %refs_0_.4), channel_id=1, source_target_pairs={{0,4},{4,0},{1,5},{5,1},{2,6},{6,2},{3,7},{7,3},{8,12},{12,8},{9,1... | collective-permute-start | bytes 786440 | tf_op jit(solution)/shard_map/ppermute | solution.py:282
  3.7 1.0 copy-done
  4.7 1.3 %pack.1 = bf16[64,9216]{1,0:T(8,128)(2,1)S(1)} custom-call(bf16[64,7168]{1,0:T(8,128)(2,1)} %refs_2_.1, bf16[128,1024]{1,0:T(8,128)(2,1)S(1)} %copy-done), custom_call_target="tpu_custom_call" | custom-call | flops 1000 | bytes 1000 | tf_op jit(solution)/shard_map/pack/pallas_call | solution.py:111
  6.0 1.6 %collective-permute-start.1 = (bf16[64,9216]{1,0:T(8,128)(2,1)S(1)}, bf16[64,9216]{1,0:T(8,128)(2,1)S(1)}, u32[]{:S(2)}, u32[]{:S(2)}) collective-permute-start(bf16[64,9216]{1,0:T(8,128)(2,1)S(1)} %pack.1), channel_id=1, source_target_pairs={{0,8},{8,0},{16,24},{24,16},{1,9},{9,1},{17,25},{25,17},{2,10},{10... | collective-permute-start | bytes 3538952 | tf_op jit(solution)/shard_map/ppermute | solution.py:304
  7.6 1.7 %collective-permute-start.4 = (bf16[64,9216]{1,0:T(8,128)(2,1)S(1)}, bf16[64,9216]{1,0:T(8,128)(2,1)}, u32[]{:S(2)}, u32[]{:S(2)}) collective-permute-start(bf16[64,9216]{1,0:T(8,128)(2,1)S(1)} %pack.1), channel_id=1, source_target_pairs={{8,16},{16,8},{9,17},{17,9},{10,18},{18,10},{11,19},{19,11},{12,20... | collective-permute-start | bytes 3538952 | tf_op jit(solution)/shard_map/ppermute | solution.py:304
  9.3 1.5 %collective-permute-start = (bf16[64,7168]{1,0:T(8,128)(2,1)}, bf16[64,7168]{1,0:T(8,128)(2,1)S(1)}, u32[]{:S(2)}, u32[]{:S(2)}) collective-permute-start(bf16[64,7168]{1,0:T(8,128)(2,1)} %refs_2_.1), channel_id=1, source_target_pairs={{2,0},{3,1},{0,2},{1,3},{6,4},{7,5},{4,6},{5,7},{10,8},{11,9},{8,1... | collective-permute-start | bytes 2752520 | tf_op jit(solution)/shard_map/ppermute | solution.py:285
  10.8 0.2 select_reduce_fusion.slot_of
  11.0 0.0 collective-permute-done.2.refs_1_
  11.0 15.6 %input_partial.1 = (bf16[64,7168]{1,0:T(8,128)(2,1)S(1)}, bf16[64,7168]{1,0:T(8,128)(2,1)S(1)}, bf16[64,7168]{1,0:T(8,128)(2,1)S(1)}, bf16[64,7168]{1,0:T(8,128)(2,1)S(1)}, bf16[7168,1024]{1,0:T(8,128)(2,1)}) custom-call(s32[448]{0:T(512)S(1)} %select_reduce_fusion.slot_of, bf16[320,128,128]{2,1,0:T(8,128)(2,1)} %bitcast.11, ...), custom_call_target="tpu_custom_call" | custom-call | flops 30064771072 | bytes 58720256 | tf_op jit(solution)/shard_map/input_partial/pallas_call | solution.py:88
  26.6 0.9 copy-done.5
  27.5 0.0 collective-permute-start.3
  27.5 3.5 %collective-permute-done.refs_1_.refs_3_ = bf16[64,7168]{1,0:T(8,128)(2,1)S(1)} collective-permute-done((bf16[64,7168]{1,0:T(8,128)(2,1)}, bf16[64,7168]{1,0:T(8,128)(2,1)S(1)}, u32[]{:S(2)}, u32[]{:S(2)}) %collective-permute-start) | collective-permute-done | bytes 917536 | tf_op jit(solution)/shard_map/ppermute | solution.py:285
  31.0 0.0 collective-permute-done.3.two
  31.0 0.4 pair_sum.1
  31.5 0.0 copy-start.4
  31.5 0.9 copy-done.4
  32.4 1.0 collective-permute-done.1.refs_6_
  33.4 0.0 collective-permute-done.4
  33.4 0.0 collective-permute-start.5
  33.5 0.5 collective-permute-start.6
  34.0 1.5 %collective-permute-start.8 = (bf16[64,7168]{1,0:T(8,128)(2,1)}, bf16[64,7168]{1,0:T(8,128)(2,1)S(1)}, u32[]{:S(2)}, u32[]{:S(2)}) collective-permute-start(bf16[64,7168]{1,0:T(8,128)(2,1)} %copy-done.4), channel_id=1, source_target_pairs={{0,2},{1,3},{2,0},{3,1},{4,6},{5,7},{6,4},{7,5},{8,10},{9,11},{10,... | collective-permute-start | bytes 2752520 | tf_op jit(solution)/shard_map/ppermute | solution.py:290
  35.5 1.3 %collective-permute-start.10 = (bf16[64,9216]{1,0:T(8,128)(2,1)}, bf16[64,9216]{1,0:T(8,128)(2,1)S(1)}, u32[]{:S(2)}, u32[]{:S(2)}) collective-permute-start(bf16[64,9216]{1,0:T(8,128)(2,1)} %collective-permute-done.4), channel_id=1, source_target_pairs={{8,0},{16,24},{9,1},{17,25},{10,2},{18,26},{11,3},{19,27},{12,4},{... | collective-permute-start | bytes 3538952 | tf_op jit(solution)/shard_map/ppermute | solution.py:304
  36.8 0.7 collective-permute-start.12
  37.5 0.0 collective-permute-done.5.refs_2_.refs_4_
  37.5 0.1 collective-permute-start.7
  37.6 0.0 collective-permute-done.6.refs_3_.refs_5_
  37.6 5.2 %copy-done.6 = bf16[7168,1024]{1,0:T(8,128)(2,1)S(1)} copy-done((bf16[7168,1024]{1,0:T(8,128)(2,1)S(1)}, bf16[7168,1024]{1,0:T(8,128)(2,1)}, u32[]{:S(2)}) %copy-start.6) | copy-done | bytes 14680088
  42.9 6.2 %output_partial.1 = bf16[256,1024]{1,0:T(8,128)(2,1)S(1)} custom-call(bf16[64,7168]{1,0:T(8,128)(2,1)} %refs_2_.1, bf16[64,7168]{1,0:T(8,128)(2,1)S(1)} %collective-permute-done.refs_1_.refs_3_, bf16[64,7168]{1,0:T(8,128)(2,1)S(1)} %collective-permute-done.5.refs_2_.refs_4_, bf16[64,7168]{1,0:T(8,128)(2,1)} %collective-permute-done.6.refs_3_.refs_5_, ...), custom_call_target="tpu_custom_call" | custom-call | flops 30064771072 | bytes 58720256 | tf_op jit(solution)/shard_map/output_partial/pallas_call | solution.py:169
  49.0 0.0 collective-permute-done.7
  49.0 7.4 %collective-permute-done.8 = bf16[64,7168]{1,0:T(8,128)(2,1)S(1)} collective-permute-done((bf16[64,7168]{1,0:T(8,128)(2,1)}, bf16[64,7168]{1,0:T(8,128)(2,1)S(1)}, u32[]{:S(2)}, u32[]{:S(2)}) %collective-permute-start.8) | collective-permute-done | bytes 917536 | tf_op jit(solution)/shard_map/ppermute | solution.py:290
  56.4 1.3 add_convert_fusion
  57.7 0.4 collective-permute-start.9
  58.1 9.4 %collective-permute-done.10 = bf16[64,9216]{1,0:T(8,128)(2,1)S(1)} collective-permute-done((bf16[64,9216]{1,0:T(8,128)(2,1)}, bf16[64,9216]{1,0:T(8,128)(2,1)S(1)}, u32[]{:S(2)}, u32[]{:S(2)}) %collective-permute-start.10) | collective-permute-done | bytes 1179680 | tf_op jit(solution)/shard_map/ppermute | solution.py:304
  67.5 0.0 collective-permute-done.12
  67.5 1.3 %collective-permute-start.13 = (bf16[64,9216]{1,0:T(8,128)(2,1)S(1)}, bf16[64,9216]{1,0:T(8,128)(2,1)S(1)}, u32[]{:S(2)}, u32[]{:S(2)}) collective-permute-start(bf16[64,9216]{1,0:T(8,128)(2,1)S(1)} %collective-permute-done.12), channel_id=1, source_target_pairs={{8,0},{16,24},{9,1},{17,25},{10,2},{18,26},{11,3},{19,27},{12,4},{... | collective-permute-start | bytes 3538952 | tf_op jit(solution)/shard_map/ppermute | solution.py:304
  68.8 1.3 %slice_select_fusion.1.refs_8_ = bf16[64,7168]{1,0:T(8,128)(2,1)S(1)} fusion(bf16[64,9216]{1,0:T(8,128)(2,1)S(1)} %collective-permute-done.10, bf16[64,9216]{1,0:T(8,128)(2,1)} %collective-permute-done.4, pred[]{:T(512)S(6)} %or.3), kind=kLoop, calls=%fused_computation.2 | loop fusion | flops 458752 | bytes 2752513 | tf_op jit(solution)/shard_map/jit(_where)/select_n | solution.py:352
  70.1 1.0 slice_select_fusion.3
  71.1 0.6 collective-permute-start.14
  71.7 0.6 collective-permute-start.11
  72.3 0.0 collective-permute-done.9
  72.3 0.8 fusion
  73.1 4.8 %weight_partial.3.refs_14_ = f32[80,128,128]{2,1,0:T(8,128)S(1)} custom-call(s32[320]{0:T(512)S(1)} %reduce.kept, bf16[128,1024]{1,0:T(8,128)(2,1)S(1)} %copy-done.1, bf16[128,1024]{1,0:T(8,128)(2,1)} %collective-permute-done.2.refs_1_, bf16[64,7168]{1,0:T(8,128)(2,1)} %refs_2_.1, bf16[64,7168]{1,0:T(8,128)(2,1)S(1)} %collective-permute-done.refs_1_.refs_3_, ...), custom_call_target="tpu_custom_call" | custom-call | flops 1000 | bytes 1000 | tf_op jit(solution)/shard_map/weight_partial/pallas_call | solution.py:251
  77.9 14.7 %collective-permute-done.14.refs_9_ = bf16[64,7168]{1,0:T(8,128)(2,1)S(1)} collective-permute-done((bf16[64,7168]{1,0:T(8,128)(2,1)S(1)}, bf16[64,7168]{1,0:T(8,128)(2,1)S(1)}, u32[]{:S(2)}, u32[]{:S(2)}) %collective-permute-start.14) | collective-permute-done | bytes 917536 | tf_op jit(solution)/shard_map/ppermute | solution.py:285
  92.6 0.0 collective-permute-start.17
  92.6 0.5 collective-permute-start.18
  93.1 4.2 %collective-permute-done.13 = bf16[64,9216]{1,0:T(8,128)(2,1)S(1)} collective-permute-done((bf16[64,9216]{1,0:T(8,128)(2,1)S(1)}, bf16[64,9216]{1,0:T(8,128)(2,1)S(1)}, u32[]{:S(2)}, u32[]{:S(2)}) %collective-permute-start.13) | collective-permute-done | bytes 1179680 | tf_op jit(solution)/shard_map/ppermute | solution.py:304
  97.3 0.1 slice_select_fusion.refs_12_
  97.4 0.1 collective-permute-start.16
  97.4 0.6 collective-permute-start.22
  98.0 0.0 collective-permute-done.18.refs_10_
  98.1 0.5 collective-permute-start.20
  98.6 0.0 collective-permute-done.11
  98.6 0.6 collective-permute-start.15
  99.2 7.7 %collective-permute-done.15.refs_5_.refs_3_ = bf16[64,2048]{1,0:T(8,128)(2,1)S(1)} collective-permute-done((bf16[64,2048]{1,0:T(8,128)(2,1)S(1)}, bf16[64,2048]{1,0:T(8,128)(2,1)S(1)}, u32[]{:S(2)}, u32[]{:S(2)}) %collective-permute-start.15) | collective-permute-done | bytes 262176 | tf_op jit(solution)/shard_map/ppermute | solution.py:282
  106.9 0.0 collective-permute-done.19.refs_11_
  107.0 0.0 collective-permute-done.20.refs_13_
  107.0 6.3 %weight_partial.4.refs_8_ = f32[80,128,128]{2,1,0:T(8,128)S(1)} custom-call(s32[320]{0:T(512)S(1)} %reduce.kept, bf16[64,2048]{1,0:T(8,128)(2,1)S(1)} %get-tuple-element.66.refs_0_, bf16[64,2048]{1,0:T(8,128)(2,1)S(1)} %get-tuple-element.64.refs_1_, bf16[64,2048]{1,0:T(8,128)(2,1)S(1)} %get-tuple-element.65.refs_2_, ...), custom_call_target="tpu_custom_call" | custom-call | flops 1000 | bytes 1000 | tf_op jit(solution)/shard_map/weight_partial/pallas_call | solution.py:251
  113.2 4.6 %collective-permute-done.16.refs_4_ = bf16[64,7168]{1,0:T(8,128)(2,1)S(1)} collective-permute-done((bf16[64,7168]{1,0:T(8,128)(2,1)S(1)}, bf16[64,7168]{1,0:T(8,128)(2,1)S(1)}, u32[]{:S(2)}, u32[]{:S(2)}) %collective-permute-start.16) | collective-permute-done | bytes 917536 | tf_op jit(solution)/shard_map/ppermute | solution.py:304
  117.9 0.0 collective-permute-start.21
  117.9 0.7 collective-permute-done.22.refs_6_
  118.5 0.0 collective-permute-start.23
  118.5 1.8 %collective-permute-done.21.refs_5_ = bf16[64,7168]{1,0:T(8,128)(2,1)S(1)} collective-permute-done((bf16[64,7168]{1,0:T(8,128)(2,1)S(1)}, bf16[64,7168]{1,0:T(8,128)(2,1)S(1)}, u32[]{:S(2)}, u32[]{:S(2)}) %collective-permute-start.21) | collective-permute-done | bytes 917536 | tf_op jit(solution)/shard_map/ppermute | solution.py:295
  120.3 1.3 %collective-permute-done.23.refs_7_ = bf16[64,7168]{1,0:T(8,128)(2,1)S(1)} collective-permute-done((bf16[64,7168]{1,0:T(8,128)(2,1)S(1)}, bf16[64,7168]{1,0:T(8,128)(2,1)S(1)}, u32[]{:S(2)}, u32[]{:S(2)}) %collective-permute-start.23) | collective-permute-done | bytes 917536 | tf_op jit(solution)/shard_map/ppermute | solution.py:295
  121.7 5.2 %weight_partial.5 = bf16[80,128,128]{2,1,0:T(8,128)(2,1)} custom-call(s32[320]{0:T(512)S(1)} %reduce.kept, bf16[64,2048]{1,0:T(8,128)(2,1)S(1)} %get-tuple-element.66.refs_0_, bf16[64,2048]{1,0:T(8,128)(2,1)S(1)} %get-tuple-element.64.refs_1_, bf16[64,2048]{1,0:T(8,128)(2,1)S(1)} %slice_select_fusion.2.refs_4_.refs_2_, ...), custom_call_target="tpu_custom_call" | custom-call | flops 1000 | bytes 1000 | tf_op jit(solution)/shard_map/weight_partial/pallas_call | solution.py:251
  (20 shorter events, 0.2 us)
Async XLA Ops:
  0.6 10.4 %collective-permute-start.2 = (bf16[128,1024]{1,0:T(8,128)(2,1)}, bf16[128,1024]{1,0:T(8,128)(2,1)}, u32[]{:S(2)}, u32[]{:S(2)}) collective-permute-start(bf16[128,1024]{1,0:T(8,128)(2,1)} %refs_0_.4), channel_id=1, source_target_pairs={{0,4},{4,0},{1,5},{5,1},{2,6},{6,2},{3,7},{7,3},{8,12},{12,8},{9,1... | collective-permute-start | bytes 786440 | tf_op jit(solution)/shard_map/ppermute | solution.py:282
  3.7 1.0 copy-start
  4.6 6.1 %copy-start.7 = (s32[1,1,320]{2,1,0:T(1,128)S(1)}, s32[1,1,320]{2,1,0:T(1,128)}, u32[]{:S(2)}) copy-start(s32[1,1,320]{2,1,0:T(1,128)} %param.6) | copy-start | bytes 3844
  4.6 6.3 %copy-start.1 = (bf16[128,1024]{1,0:T(8,128)(2,1)S(1)}, bf16[128,1024]{1,0:T(8,128)(2,1)}, u32[]{:S(2)}) copy-start(bf16[128,1024]{1,0:T(8,128)(2,1)} %refs_0_.4) | copy-start | bytes 786436
  6.0 27.5 %collective-permute-start.1 = (bf16[64,9216]{1,0:T(8,128)(2,1)S(1)}, bf16[64,9216]{1,0:T(8,128)(2,1)S(1)}, u32[]{:S(2)}, u32[]{:S(2)}) collective-permute-start(bf16[64,9216]{1,0:T(8,128)(2,1)S(1)} %pack.1), channel_id=1, source_target_pairs={{0,8},{8,0},{16,24},{24,16},{1,9},{9,1},{17,25},{25,17},{2,10},{10... | collective-permute-start | bytes 3538952 | tf_op jit(solution)/shard_map/ppermute | solution.py:304
  7.6 25.9 %collective-permute-start.4 = (bf16[64,9216]{1,0:T(8,128)(2,1)S(1)}, bf16[64,9216]{1,0:T(8,128)(2,1)}, u32[]{:S(2)}, u32[]{:S(2)}) collective-permute-start(bf16[64,9216]{1,0:T(8,128)(2,1)S(1)} %pack.1), channel_id=1, source_target_pairs={{8,16},{16,8},{9,17},{17,9},{10,18},{18,10},{11,19},{19,11},{12,20... | collective-permute-start | bytes 3538952 | tf_op jit(solution)/shard_map/ppermute | solution.py:304
  9.3 21.7 %collective-permute-start = (bf16[64,7168]{1,0:T(8,128)(2,1)}, bf16[64,7168]{1,0:T(8,128)(2,1)S(1)}, u32[]{:S(2)}, u32[]{:S(2)}) collective-permute-start(bf16[64,7168]{1,0:T(8,128)(2,1)} %refs_2_.1), channel_id=1, source_target_pairs={{2,0},{3,1},{0,2},{1,3},{6,4},{7,5},{4,6},{5,7},{10,8},{11,9},{8,1... | collective-permute-start | bytes 2752520 | tf_op jit(solution)/shard_map/ppermute | solution.py:285
  26.6 0.9 copy-start.5
  27.5 4.0 %copy-start.2 = (bf16[64,7168]{1,0:T(8,128)(2,1)}, bf16[64,7168]{1,0:T(8,128)(2,1)S(1)}, u32[]{:S(2)}) copy-start(bf16[64,7168]{1,0:T(8,128)(2,1)S(1)} %get-tuple-element.43) | copy-start | bytes 2752516
  27.5 3.5 %collective-permute-start.3 = (bf16[64,7168]{1,0:T(8,128)(2,1)S(1)}, bf16[64,7168]{1,0:T(8,128)(2,1)S(1)}, u32[]{:S(2)}, u32[]{:S(2)}) collective-permute-start(bf16[64,7168]{1,0:T(8,128)(2,1)S(1)} %get-tuple-element.35), channel_id=1, source_target_pairs={{0,1},{1,0},{2,3},{3,2},{4,5},{5,4},{6,7},{7,6},{8,9},{9,8},{10,11... | collective-permute-start | bytes 2752520 | tf_op jit(solution)/shard_map/ppermute | solution.py:295
  31.5 0.9 copy-start.4
  33.4 4.1 %collective-permute-start.5 = (bf16[64,7168]{1,0:T(8,128)(2,1)}, bf16[64,7168]{1,0:T(8,128)(2,1)S(1)}, u32[]{:S(2)}, u32[]{:S(2)}) collective-permute-start(bf16[64,7168]{1,0:T(8,128)(2,1)} %refs_2_.1), channel_id=1, source_target_pairs={{0,1},{1,0},{2,3},{3,2},{4,5},{5,4},{6,7},{7,6},{8,9},{9,8},{10,11... | collective-permute-start | bytes 2752520 | tf_op jit(solution)/shard_map/ppermute | solution.py:295
  33.5 4.2 %collective-permute-start.6 = (bf16[64,7168]{1,0:T(8,128)(2,1)S(1)}, bf16[64,7168]{1,0:T(8,128)(2,1)}, u32[]{:S(2)}, u32[]{:S(2)}) collective-permute-start(bf16[64,7168]{1,0:T(8,128)(2,1)S(1)} %collective-permute-done.refs_1_.refs_3_), channel_id=1, source_target_pairs={{0,1},{1,0},{2,3},{3,2},{4,5},{5,4},{6,7},{7,6},{8,9},{9,8},{10,11... | collective-permute-start | bytes 2752520 | tf_op jit(solution)/shard_map/ppermute | solution.py:295
  34.0 22.5 %collective-permute-start.8 = (bf16[64,7168]{1,0:T(8,128)(2,1)}, bf16[64,7168]{1,0:T(8,128)(2,1)S(1)}, u32[]{:S(2)}, u32[]{:S(2)}) collective-permute-start(bf16[64,7168]{1,0:T(8,128)(2,1)} %copy-done.4), channel_id=1, source_target_pairs={{0,2},{1,3},{2,0},{3,1},{4,6},{5,7},{6,4},{7,5},{8,10},{9,11},{10,... | collective-permute-start | bytes 2752520 | tf_op jit(solution)/shard_map/ppermute | solution.py:290
  35.5 32.0 %collective-permute-start.10 = (bf16[64,9216]{1,0:T(8,128)(2,1)}, bf16[64,9216]{1,0:T(8,128)(2,1)S(1)}, u32[]{:S(2)}, u32[]{:S(2)}) collective-permute-start(bf16[64,9216]{1,0:T(8,128)(2,1)} %collective-permute-done.4), channel_id=1, source_target_pairs={{8,0},{16,24},{9,1},{17,25},{10,2},{18,26},{11,3},{19,27},{12,4},{... | collective-permute-start | bytes 3538952 | tf_op jit(solution)/shard_map/ppermute | solution.py:304
  36.8 30.7 %collective-permute-start.12 = (bf16[64,9216]{1,0:T(8,128)(2,1)S(1)}, bf16[64,9216]{1,0:T(8,128)(2,1)S(1)}, u32[]{:S(2)}, u32[]{:S(2)}) collective-permute-start(bf16[64,9216]{1,0:T(8,128)(2,1)S(1)} %collective-permute-done.1.refs_6_), channel_id=1, source_target_pairs={{8,16},{16,8},{9,17},{17,9},{10,18},{18,10},{11,19},{19,11},{12,20... | collective-permute-start | bytes 3538952 | tf_op jit(solution)/shard_map/ppermute | solution.py:304
  37.5 18.9 %copy-start.3 = (bf16[64,7168]{1,0:T(8,128)(2,1)S(1)}, bf16[64,7168]{1,0:T(8,128)(2,1)}, u32[]{:S(2)}) copy-start(bf16[64,7168]{1,0:T(8,128)(2,1)} %copy-done.2) | copy-start | bytes 2752516
  37.5 11.5 %collective-permute-start.7 = (bf16[64,7168]{1,0:T(8,128)(2,1)}, bf16[64,7168]{1,0:T(8,128)(2,1)S(1)}, u32[]{:S(2)}, u32[]{:S(2)}) collective-permute-start(bf16[64,7168]{1,0:T(8,128)(2,1)} %copy-done.5), channel_id=1, source_target_pairs={{0,1},{1,0},{2,3},{3,2},{4,5},{5,4},{6,7},{7,6},{8,9},{9,8},{10,11... | collective-permute-start | bytes 2752520 | tf_op jit(solution)/shard_map/ppermute | solution.py:295
  37.6 5.2 %copy-start.6 = (bf16[7168,1024]{1,0:T(8,128)(2,1)S(1)}, bf16[7168,1024]{1,0:T(8,128)(2,1)}, u32[]{:S(2)}) copy-start(bf16[7168,1024]{1,0:T(8,128)(2,1)} %get-tuple-element.42.refs_4_) | copy-start | bytes 44040196
  57.7 14.6 %collective-permute-start.9 = (bf16[128,1024]{1,0:T(8,128)(2,1)S(1)}, bf16[128,1024]{1,0:T(8,128)(2,1)S(1)}, u32[]{:S(2)}, u32[]{:S(2)}) collective-permute-start(bf16[128,1024]{1,0:T(8,128)(2,1)S(1)} %dynamic-slice_bitcast_fusion), channel_id=1, source_target_pairs={{0,4},{4,0},{1,5},{5,1},{2,6},{6,2},{3,7},{7,3},{8,12},{12,8},{9,1... | collective-permute-start | bytes 786440 | tf_op jit(solution)/shard_map/ppermute | solution.py:282
  67.5 29.8 %collective-permute-start.13 = (bf16[64,9216]{1,0:T(8,128)(2,1)S(1)}, bf16[64,9216]{1,0:T(8,128)(2,1)S(1)}, u32[]{:S(2)}, u32[]{:S(2)}) collective-permute-start(bf16[64,9216]{1,0:T(8,128)(2,1)S(1)} %collective-permute-done.12), channel_id=1, source_target_pairs={{8,0},{16,24},{9,1},{17,25},{10,2},{18,26},{11,3},{19,27},{12,4},{... | collective-permute-start | bytes 3538952 | tf_op jit(solution)/shard_map/ppermute | solution.py:304
  71.1 21.5 %collective-permute-start.14 = (bf16[64,7168]{1,0:T(8,128)(2,1)S(1)}, bf16[64,7168]{1,0:T(8,128)(2,1)S(1)}, u32[]{:S(2)}, u32[]{:S(2)}) collective-permute-start(bf16[64,7168]{1,0:T(8,128)(2,1)S(1)} %slice_select_fusion.1.refs_8_), channel_id=1, source_target_pairs={{2,0},{3,1},{0,2},{1,3},{6,4},{7,5},{4,6},{5,7},{10,8},{11,9},{8,1... | collective-permute-start | bytes 2752520 | tf_op jit(solution)/shard_map/ppermute | solution.py:285
  71.7 26.8 %collective-permute-start.11 = (bf16[128,2048]{1,0:T(8,128)(2,1)S(1)}, bf16[128,2048]{1,0:T(8,128)(2,1)S(1)}, u32[]{:S(2)}, u32[]{:S(2)}) collective-permute-start(bf16[128,2048]{1,0:T(8,128)(2,1)S(1)} %pad_maximum_fusion), channel_id=1, source_target_pairs={{0,4},{4,0},{1,5},{5,1},{2,6},{6,2},{3,7},{7,3},{8,12},{12,8},{9,1... | collective-permute-start | bytes 1572872 | tf_op jit(solution)/shard_map/ppermute | solution.py:282
  92.6 5.5 %collective-permute-start.17 = (bf16[64,9216]{1,0:T(8,128)(2,1)S(1)}, bf16[64,9216]{1,0:T(8,128)(2,1)S(1)}, u32[]{:S(2)}, u32[]{:S(2)}) collective-permute-start(bf16[64,9216]{1,0:T(8,128)(2,1)S(1)} %collective-permute-done.1.refs_6_), channel_id=1, source_target_pairs={{0,1},{1,0},{2,3},{3,2},{4,5},{5,4},{6,7},{7,6},{8,9},{9,8},{10,11... | collective-permute-start | bytes 3538952 | tf_op jit(solution)/shard_map/ppermute | solution.py:295
  92.6 5.5 %collective-permute-start.18 = (bf16[64,7168]{1,0:T(8,128)(2,1)S(1)}, bf16[64,7168]{1,0:T(8,128)(2,1)S(1)}, u32[]{:S(2)}, u32[]{:S(2)}) collective-permute-start(bf16[64,7168]{1,0:T(8,128)(2,1)S(1)} %slice_select_fusion.1.refs_8_), channel_id=1, source_target_pairs={{0,1},{1,0},{2,3},{3,2},{4,5},{5,4},{6,7},{7,6},{8,9},{9,8},{10,11... | collective-permute-start | bytes 2752520 | tf_op jit(solution)/shard_map/ppermute | solution.py:295
  97.4 20.5 %collective-permute-start.16 = (bf16[64,7168]{1,0:T(8,128)(2,1)S(1)}, bf16[64,7168]{1,0:T(8,128)(2,1)S(1)}, u32[]{:S(2)}, u32[]{:S(2)}) collective-permute-start(bf16[64,7168]{1,0:T(8,128)(2,1)S(1)} %collective-permute-done.refs_1_.refs_3_), channel_id=1, source_target_pairs={{0,8},{8,0},{16,24},{24,16},{1,9},{9,1},{17,25},{25,17},{2,10},{10... | collective-permute-start | bytes 2752520 | tf_op jit(solution)/shard_map/ppermute | solution.py:304
  97.4 21.1 %collective-permute-start.22 = (bf16[64,7168]{1,0:T(8,128)(2,1)S(1)}, bf16[64,7168]{1,0:T(8,128)(2,1)S(1)}, u32[]{:S(2)}, u32[]{:S(2)}) collective-permute-start(bf16[64,7168]{1,0:T(8,128)(2,1)S(1)} %slice_select_fusion.refs_12_), channel_id=1, source_target_pairs={{2,0},{3,1},{0,2},{1,3},{6,4},{7,5},{4,6},{5,7},{10,8},{11,9},{8,1... | collective-permute-start | bytes 2752520 | tf_op jit(solution)/shard_map/ppermute | solution.py:285
  98.0 8.9 %collective-permute-start.19 = (bf16[64,7168]{1,0:T(8,128)(2,1)S(1)}, bf16[64,7168]{1,0:T(8,128)(2,1)S(1)}, u32[]{:S(2)}, u32[]{:S(2)}) collective-permute-start(bf16[64,7168]{1,0:T(8,128)(2,1)S(1)} %collective-permute-done.14.refs_9_), channel_id=1, source_target_pairs={{0,1},{1,0},{2,3},{3,2},{4,5},{5,4},{6,7},{7,6},{8,9},{9,8},{10,11... | collective-permute-start | bytes 2752520 | tf_op jit(solution)/shard_map/ppermute | solution.py:295
  98.1 8.9 %collective-permute-start.20 = (bf16[64,7168]{1,0:T(8,128)(2,1)S(1)}, bf16[64,7168]{1,0:T(8,128)(2,1)S(1)}, u32[]{:S(2)}, u32[]{:S(2)}) collective-permute-start(bf16[64,7168]{1,0:T(8,128)(2,1)S(1)} %slice_select_fusion.refs_12_), channel_id=1, source_target_pairs={{0,1},{1,0},{2,3},{3,2},{4,5},{5,4},{6,7},{7,6},{8,9},{9,8},{10,11... | collective-permute-start | bytes 2752520 | tf_op jit(solution)/shard_map/ppermute | solution.py:295
  98.6 8.3 %collective-permute-start.15 = (bf16[64,2048]{1,0:T(8,128)(2,1)S(1)}, bf16[64,2048]{1,0:T(8,128)(2,1)S(1)}, u32[]{:S(2)}, u32[]{:S(2)}) collective-permute-start(bf16[64,2048]{1,0:T(8,128)(2,1)S(1)} %slice_select_fusion.2.refs_4_.refs_2_), channel_id=1, source_target_pairs={{0,4},{4,0},{1,5},{5,1},{2,6},{6,2},{3,7},{7,3},{8,12},{12,8},{9,1... | collective-permute-start | bytes 786440 | tf_op jit(solution)/shard_map/ppermute | solution.py:282
  117.9 2.5 %collective-permute-start.21 = (bf16[64,7168]{1,0:T(8,128)(2,1)S(1)}, bf16[64,7168]{1,0:T(8,128)(2,1)S(1)}, u32[]{:S(2)}, u32[]{:S(2)}) collective-permute-start(bf16[64,7168]{1,0:T(8,128)(2,1)S(1)} %collective-permute-done.16.refs_4_), channel_id=1, source_target_pairs={{0,1},{1,0},{2,3},{3,2},{4,5},{5,4},{6,7},{7,6},{8,9},{9,8},{10,11... | collective-permute-start | bytes 2752520 | tf_op jit(solution)/shard_map/ppermute | solution.py:295
  118.5 3.1 %collective-permute-start.23 = (bf16[64,7168]{1,0:T(8,128)(2,1)S(1)}, bf16[64,7168]{1,0:T(8,128)(2,1)S(1)}, u32[]{:S(2)}, u32[]{:S(2)}) collective-permute-start(bf16[64,7168]{1,0:T(8,128)(2,1)S(1)} %collective-permute-done.22.refs_6_), channel_id=1, source_target_pairs={{0,1},{1,0},{2,3},{3,2},{4,5},{5,4},{6,7},{7,6},{8,9},{9,8},{10,11... | collective-permute-start | bytes 2752520 | tf_op jit(solution)/shard_map/ppermute | solution.py:295
